TPU v7x, 128 devices: a whole 4x4x4 slice. The times are simulated.
128 devices in a mesh: prow: 8 (over y_hi, z), pcol: 16 (over x, y_lo, core).
Axes of the slice: x: 4, y: 4 (y_hi: 2, y_lo: 2; y = y_hi * 2 + y_lo), z: 4, core: 2. Of those that a mesh axis runs over, the one named last changes fastest.
Arguments:
- front_entries: float32 [12288, 12288], P('prow', 'pcol'), may hold values from -6 to 6
- diagonal: float32 [12288], replicated, may hold values from 120 to 240
- child_update: float32 [16384, 8192], P('prow', 'pcol'), may hold values from -6 to 6
- child_map: int32 [2, 64], replicated, may hold values from 0 to 95, as said below
Outputs:
- factored: float32 [12288, 12288], P('prow', 'pcol')
Inputs may be any that keep to these rules, and one draw needn't show every extreme that they name: Each row of child_map names 64 distinct front blocks, and child_map[c, k] mod 16 = (k + r_c) mod 16 for a shift r_c of child c.
All inputs are finite; a program needn't handle non-finite values.
Results may differ from a plain program's by a relative error of at most 0.0001.
Values sent between devices are 32-bit elements; how exact they have to be, the bound alone decides.
No kernel may reach another device: no remote copies, remote signals or barrier semaphores. Data moves between devices by JAX's collectives and lax.ppermute only.
A program may use at most 192 MiB of HBM per device.

v0:
```python
import jax
import jax.numpy as jnp
from jax import lax
from jax.sharding import PartitionSpec as P

FRONT = 12288
CHILD = 8192
BLOCK = 128
PANEL = 512
PANELS = 2


HIGHEST = lax.Precision.HIGHEST


def broadcast(shard, axis, root):
    mine = lax.axis_index(axis) == root
    return lax.psum(jnp.where(mine, shard, jnp.zeros_like(shard)), axis)


def one_hot(values, number):
    return (values[..., None] == jnp.arange(number)[None]).astype(jnp.float32)


def per_device(front_entries, diagonal, child_update, child_map):
    row_procs = lax.axis_size("prow")
    col_procs = lax.axis_size("pcol")
    my_row = lax.axis_index("prow")
    my_col = lax.axis_index("pcol")
    group_rows = row_procs // 2
    front_blocks = FRONT // BLOCK
    child_blocks = CHILD // BLOCK
    panel_blocks = PANEL // BLOCK
    local_rows = front_blocks // row_procs
    local_cols = front_blocks // col_procs
    slab_blocks = child_blocks // group_rows
    row_send = slab_blocks // row_procs
    col_blocks = child_blocks // col_procs
    by_source = child_map.reshape(row_procs, slab_blocks)
    sorting = jnp.argsort(by_source % row_procs, axis=1, stable=True)
    sorted_targets = jnp.take_along_axis(by_source, sorting, axis=1)
    my_sorting = lax.dynamic_index_in_dim(sorting, my_row, 0, keepdims=False)
    received_rows = lax.dynamic_slice_in_dim(sorted_targets, my_row * row_send, row_send, 1)
    row_place = one_hot(received_rows // row_procs, local_rows).reshape(
        2, group_rows, row_send, local_rows
    )
    col_targets = child_map.reshape(2, col_procs, col_blocks)
    col_owner = one_hot(col_targets % col_procs, col_procs)
    mine_col = lax.dynamic_index_in_dim(col_owner, my_col, 1, keepdims=False)
    arrivals = lax.dynamic_index_in_dim(col_owner, my_col, 3, keepdims=False)
    col_place = jnp.einsum(
        "cbm,cbms->cbs", arrivals, one_hot(col_targets // col_procs, local_cols), precision=HIGHEST
    )
    rows_sorted = child_update.reshape(slab_blocks, BLOCK, col_blocks * BLOCK)[my_sorting]
    rows_sorted = rows_sorted.reshape(row_procs, row_send, BLOCK, col_blocks, BLOCK)
    first_section = lax.all_to_all(
        rows_sorted.reshape(row_procs, row_send * BLOCK, col_blocks * BLOCK),
        "prow",
        split_axis=0,
        concat_axis=0,
        tiled=True,
    )
    first_section = first_section.reshape(2, group_rows, row_send, BLOCK, col_blocks, BLOCK)
    outgoing = jnp.einsum("cmq,chnxmy->qchnxy", mine_col, first_section, precision=HIGHEST)
    outgoing = outgoing.reshape(col_procs, row_procs * row_send * BLOCK, BLOCK)
    incoming = lax.all_to_all(outgoing, "pcol", split_axis=0, concat_axis=0, tiled=True)
    incoming = incoming.reshape(col_procs, 2, group_rows, row_send, BLOCK, BLOCK)
    gathered_rows = jnp.einsum("chnl,bchnxy->clbxy", row_place, incoming, precision=HIGHEST)
    extended = jnp.einsum("cbs,clbxy->lxsy", col_place, gathered_rows, precision=HIGHEST)
    row_ids = jnp.arange(local_rows) * row_procs + my_row
    col_ids = jnp.arange(local_cols) * col_procs + my_col
    diag_values = lax.dynamic_index_in_dim(
        diagonal.reshape(local_cols, col_procs, BLOCK), my_col, 1, keepdims=False
    )
    on_diagonal = (row_ids[:, None] == col_ids[None, :]).astype(jnp.float32)
    identity = jnp.eye(BLOCK, dtype=jnp.float32)
    diag_part = (
        on_diagonal[:, None, :, None] * identity[None, :, None, :] * diag_values[None, None, :, :]
    )
    blocked = front_entries.reshape(local_rows, BLOCK, local_cols, BLOCK) + diag_part + extended
    matrix = blocked.reshape(local_rows * BLOCK, local_cols * BLOCK)
    stride_blocks = col_procs // row_procs
    for panel_index in range(PANELS):
        first_block = panel_index * panel_blocks
        after_block = first_block + panel_blocks
        columns = []
        for offset in range(panel_blocks):
            global_block = first_block + offset
            column_start = global_block // col_procs * BLOCK
            columns.append(
                broadcast(
                    matrix[:, column_start : column_start + BLOCK], "pcol", global_block % col_procs
                )
            )
        panel_rows = jnp.concatenate(columns, axis=1)
        pieces = []
        for offset in range(panel_blocks):
            global_block = first_block + offset
            row_start = global_block // row_procs * BLOCK
            pieces.append(
                broadcast(
                    panel_rows[row_start : row_start + BLOCK], "prow", global_block % row_procs
                )
            )
        pivot_block = jnp.concatenate(pieces, axis=0)
        pivot_block = 0.5 * (pivot_block + pivot_block.T)
        factor = jnp.linalg.cholesky(pivot_block)
        solved = lax.linalg.triangular_solve(
            factor, panel_rows, left_side=False, lower=True, transpose_a=True
        )
        inside = (row_ids >= first_block) & (row_ids < after_block)
        beyond = row_ids >= after_block
        chosen = jnp.clip(row_ids - first_block, 0, panel_blocks - 1)
        factor_rows = factor.reshape(panel_blocks, BLOCK, PANEL)[chosen]
        trailing = jnp.where(beyond[:, None, None], solved.reshape(local_rows, BLOCK, PANEL), 0.0)
        lower_panel = jnp.where(inside[:, None, None], factor_rows, trailing)
        trailing = trailing.reshape(local_rows * BLOCK, PANEL)
        candidates = trailing.reshape(local_cols, stride_blocks, BLOCK, PANEL)
        offered = lax.dynamic_index_in_dim(candidates, my_col // row_procs, 1, keepdims=False)
        offered = offered.reshape(local_cols * BLOCK, PANEL)
        col_panel = broadcast(offered, "prow", my_col % row_procs)
        matrix = matrix - jnp.einsum("ik,jk->ij", trailing, col_panel, precision=HIGHEST)
        col_inside = (col_ids >= first_block) & (col_ids < after_block)
        col_beyond = col_ids >= after_block
        col_chosen = jnp.clip(col_ids - first_block, 0, panel_blocks - 1)
        lower_cols = lower_panel.reshape(local_rows, BLOCK, panel_blocks, BLOCK)[
            :, :, col_chosen, :
        ]
        blocked = matrix.reshape(local_rows, BLOCK, local_cols, BLOCK)
        blocked = jnp.where(col_inside[None, None, :, None], lower_cols, blocked)
        blocked = jnp.where(
            inside[:, None, None, None] & col_beyond[None, None, :, None], 0.0, blocked
        )
        matrix = blocked.reshape(local_rows * BLOCK, local_cols * BLOCK)
    return matrix


def solution(mesh):
    return jax.shard_map(
        per_device,
        mesh=mesh,
        in_specs=(P("prow", "pcol"), P(), P("prow", "pcol"), P()),
        out_specs=P("prow", "pcol"),
        check_vma=False,
    )
```

profile of v0, /device:TPU:0, one launch (start us, length us, event | category | flops | bytes accessed | tf_op | source)
XLA Modules:
  0.0 1459.6 jit_solution(9704673471707823878)
XLA Ops:
  22.0 48.5 %all-to-all-done = f32[8,256,512]{2,1,0:T(8,128)} async-done(((f32[8,256,512]{2,1,0:T(8,128)}), f32[8,256,512]{2,1,0:T(8,128)}, u32[]{:S(2)}, u32[]{:S(2)}) %all-to-all-start) | async-done | bytes 4194336 | tf_op jit(solution)/shard_map/all_to_all | solution.py:56
  75.7 8.9 fusion.92
  84.6 10.6 copy.65
  109.2 262.7 %all-to-all-done.1 = f32[16,2048,128]{2,1,0:T(8,128)} async-done(((f32[16,2048,128]{2,1,0:T(8,128)}), f32[16,2048,128]{2,1,0:T(8,128)}, u32[]{:S(2)}, u32[]{:S(2)}) %all-to-all-start.1) | async-done | bytes 16777248 | tf_op jit(solution)/shard_map/all_to_all | solution.py:66
  371.8 55.5 %convolution_bitcast_fusion = f32[2,12,16,128,128]{4,1,3,2,0:T(8,128)} fusion(f32[16,2,4,2,128,128]{5,4,3,2,1,0:T(8,128)} %bitcast.15, pred[2,4,2,12,1,1]{3,2,1,5,4,0:T(4,128)(4,1)S(1)} %fusion.126), kind=kOutput, calls=%fused_computation.12 | convolution fusion | flops 603979776 | bytes 41943232 | tf_op jit(solution)/shard_map/chnl,bchnxy->clbxy/dot_general | solution.py:68
  427.4 33.7 %bitcast_add_fusion = f32[12,128,6,128]{3,2,1,0:T(8,128)S(1)} fusion(f32[12,128,6,128]{3,2,1,0:T(8,128)S(1)} %copy-done.2, f32[6,128]{1,0:T(8,128)S(1)} %bitcast.254, f32[128,128]{1,0:T(8,128)S(1)} %fusion.73, f32[12,6]{1,0:T(8,128)S(1)} %compare_convert_fusion, f32[2,12,16,128,128]{4,1,3,2,0:T(8,128)} %convolution_bitcast_fusion, ...), kind=kOutput, calls=%fused_computation.14 | convolution fusion | flops 457703424 | bytes 34672672 | tf_op jit(solution)/shard_map/cbs,clbxy->lxsy/dot_general | solution.py:69
  466.3 128.2 %all-reduce.18.cloned.1.call-done = (f32[1536,128]{1,0:T(8,128)}, f32[1536,128]{1,0:T(8,128)}, f32[1536,128]{1,0:T(8,128)}, f32[1536,128]{1,0:T(8,128)}) async-done(((f32[1536,128]{1,0:T(8,128)}, f32[1536,128]{1,0:T(8,128)}, f32[1536,128]{1,0:T(8,128)}, f32[1536,128]{1,0:T(8,128)}), (f32[1536,128]{1,0:T(8,128)}, f32[1536,128]{1,0:T(8,128)}, f32[1536,128]{1,0:T(8,128)}, ...) | async-done | bytes 3145744 | tf_op jit(solution)/shard_map/psum | solution.py:18
  597.5 88.2 %all-reduce.22.cloned.1.call-done = (f32[128,512]{1,0:T(8,128)}, f32[128,512]{1,0:T(8,128)}, f32[128,512]{1,0:T(8,128)}, f32[128,512]{1,0:T(8,128)}) async-done(((f32[128,512]{1,0:T(8,128)}, f32[128,512]{1,0:T(8,128)}, f32[128,512]{1,0:T(8,128)}, f32[128,512]{1,0:T(8,128)}), (f32[128,512]{1,0:T(8,128)}, f32[128,512]{1,0:T(8,128)}, f32[128,512]{1,0:T(8,128)}, ...) | async-done | bytes 1048592 | tf_op jit(solution)/shard_map/psum | solution.py:18
  690.8 11.7 cholesky.286
  702.6 9.8 custom-call.29
  713.1 11.7 cholesky.305
  724.9 10.2 custom-call.30
  735.7 11.7 cholesky.326
  748.1 9.8 custom-call.31
  759.5 11.8 cholesky.343
  776.7 11.7 while.4
  788.4 39.3 %custom-call.32 = f32[4,128,128]{1,2,0:T(8,128)S(1)} custom-call(f32[4,128,128]{2,1,0:T(8,128)S(1)} %get-tuple-element.23), custom_call_target="InvertDiagBlocksLowerTriangular" | custom-call | tf_op jit(solution)/shard_map/triangular_solve/custom-call.3 | solution.py:108
  885.9 58.7 %all-reduce.12.cloned.1.call-done = f32[768,512]{0,1:T(8,128)} async-done(((f32[768,512]{0,1:T(8,128)}), f32[768,512]{0,1:T(8,128)}) %all-reduce.12.cloned.1.call-update) | async-done | bytes 1572880 | tf_op jit(solution)/shard_map/psum | solution.py:18
  945.1 12.9 fusion.4
  962.0 125.7 %all-reduce.16.cloned.1.call-done = (f32[1536,128]{1,0:T(8,128)}, f32[1536,128]{1,0:T(8,128)}, f32[1536,128]{1,0:T(8,128)}, f32[1536,128]{1,0:T(8,128)}) async-done(((f32[1536,128]{1,0:T(8,128)}, f32[1536,128]{1,0:T(8,128)}, f32[1536,128]{1,0:T(8,128)}, f32[1536,128]{1,0:T(8,128)}), (f32[1536,128]{1,0:T(8,128)}, f32[1536,128]{1,0:T(8,128)}, f32[1536,128]{1,0:T(8,128)}, ...) | async-done | bytes 3145744 | tf_op jit(solution)/shard_map/psum | solution.py:18
  1090.6 88.3 %all-reduce.20.cloned.1.call-done = (f32[128,512]{1,0:T(8,128)}, f32[128,512]{1,0:T(8,128)}, f32[128,512]{1,0:T(8,128)}, f32[128,512]{1,0:T(8,128)}) async-done(((f32[128,512]{1,0:T(8,128)}, f32[128,512]{1,0:T(8,128)}, f32[128,512]{1,0:T(8,128)}, f32[128,512]{1,0:T(8,128)}), (f32[128,512]{1,0:T(8,128)}, f32[128,512]{1,0:T(8,128)}, f32[128,512]{1,0:T(8,128)}, ...) | async-done | bytes 1048592 | tf_op jit(solution)/shard_map/psum | solution.py:18
  1184.4 11.7 cholesky.358
  1196.3 9.8 custom-call.33
  1206.8 11.7 cholesky.377
  1219.8 10.2 custom-call.34
  1230.6 11.7 cholesky.398
  1243.1 9.8 custom-call.35
  1254.4 11.9 cholesky.415
  1271.0 11.1 while.5
  1282.1 39.3 %custom-call.36 = f32[4,128,128]{1,2,0:T(8,128)S(1)} custom-call(f32[4,128,128]{2,1,0:T(8,128)S(1)} %get-tuple-element.24), custom_call_target="InvertDiagBlocksLowerTriangular" | custom-call | tf_op jit(solution)/shard_map/triangular_solve/custom-call.3 | solution.py:108
  1379.3 58.8 %all-reduce.14.cloned.1.call-done = f32[768,512]{0,1:T(8,128)} async-done(((f32[768,512]{0,1:T(8,128)}), f32[768,512]{0,1:T(8,128)}) %all-reduce.14.cloned.1.call-update) | async-done | bytes 1572880 | tf_op jit(solution)/shard_map/psum | solution.py:18
  1438.7 13.6 fusion.3
  (270 shorter events, 213.0 us)
Async XLA Ops:
  6.5 95.7 %copy-start = (f32[12288]{0:T(1024)S(1)}, f32[12288]{0:T(1024)}, u32[]{:S(2)}) copy-start(f32[12288]{0:T(1024)} %param.8) | copy-start | bytes 147460
  13.3 8.2 copy-start.33
  13.3 57.1 %all-to-all-start = ((f32[8,256,512]{2,1,0:T(8,128)}), f32[8,256,512]{2,1,0:T(8,128)}, u32[]{:S(2)}, u32[]{:S(2)}) async-start(f32[8,256,512]{2,1,0:T(8,128)} %bitcast.240), calls=%async_computation | async-start | bytes 8388608 | tf_op jit(solution)/shard_map/all_to_all | solution.py:56
  95.2 276.6 %all-to-all-start.1 = ((f32[16,2048,128]{2,1,0:T(8,128)}), f32[16,2048,128]{2,1,0:T(8,128)}, u32[]{:S(2)}, u32[]{:S(2)}) async-start(f32[16,2048,128]{2,1,0:T(8,128)} %copy.65), calls=%async_computation.1 | async-start | bytes 33554432 | tf_op jit(solution)/shard_map/all_to_all | solution.py:66
  100.4 494.1 %all-reduce.18.cloned.1.call-start = ((), (), s32[]{:S(2)}) async-start(), calls=%async_computation.5 | async-start | bytes 6291456 | tf_op jit(solution)/shard_map/psum | solution.py:18
  371.8 55.5 %copy-start.2 = (f32[12,128,6,128]{3,2,1,0:T(8,128)S(1)}, f32[12,128,6,128]{3,2,1,0:T(8,128)}, u32[]{:S(2)}) copy-start(f32[12,128,6,128]{3,2,1,0:T(8,128)} %reshape.441) | copy-start | bytes 14155780
  466.2 219.5 %all-reduce.22.cloned.1.call-start = ((), (), s32[]{:S(2)}) async-start(), calls=%async_computation.7 | async-start | bytes 2097152 | tf_op jit(solution)/shard_map/psum | solution.py:18
  597.1 347.5 %all-reduce.12.cloned.1.call-start = ((), (), s32[]{:S(2)}) async-start(), calls=%async_computation.2 | async-start | bytes 3145728 | tf_op jit(solution)/shard_map/psum | solution.py:18
  690.7 67.2 %copy-start.31 = (f32[512,512]{1,0:T(8,128)}, f32[512,512]{1,0:T(8,128)S(1)}, u32[]{:S(2)}) copy-start(f32[512,512]{1,0:T(8,128)S(1)} %fusion.32) | copy-start | bytes 3145732
  724.9 102.9 %copy-start.22 = (f32[1536,128]{1,0:T(8,128)S(1)}, f32[1536,128]{1,0:T(8,128)}, u32[]{:S(2)}) copy-start(f32[1536,128]{1,0:T(8,128)} %get-tuple-element.48) | copy-start | bytes 2359300
  758.2 70.5 %copy-start.25 = (f32[1536,128]{1,0:T(8,128)S(1)}, f32[1536,128]{1,0:T(8,128)}, u32[]{:S(2)}) copy-start(f32[1536,128]{1,0:T(8,128)} %get-tuple-element.47) | copy-start | bytes 2359300
  776.7 55.1 %copy-start.24 = (f32[1536,128]{1,0:T(8,128)S(1)}, f32[1536,128]{1,0:T(8,128)}, u32[]{:S(2)}) copy-start(f32[1536,128]{1,0:T(8,128)} %get-tuple-element.46) | copy-start | bytes 2359300
  828.6 14.0 copy-start.5
  831.9 10.8 copy-start.11
  856.0 231.7 %all-reduce.16.cloned.1.call-start = ((), (), s32[]{:S(2)}) async-start(), calls=%async_computation.4 | async-start | bytes 6291456 | tf_op jit(solution)/shard_map/psum | solution.py:18
  877.8 67.2 %copy-start.6 = (f32[128,1536]{1,0:T(8,128)S(1)}, f32[128,1536]{1,0:T(8,128)}, u32[]{:S(2)}) copy-start(f32[128,1536]{1,0:T(8,128)} %copy-done.5) | copy-start | bytes 2359300
  877.8 67.2 %copy-start.12 = (f32[1536,128]{0,1:T(8,128)S(1)}, f32[1536,128]{0,1:T(8,128)}, u32[]{:S(2)}) copy-start(f32[1536,128]{0,1:T(8,128)} %copy-done.11) | copy-start | bytes 2359300
  877.8 67.3 %copy-start.16 = (f32[1536,128]{0,1:T(8,128)S(1)}, f32[1536,128]{0,1:T(8,128)}, u32[]{:S(2)}) copy-start(f32[1536,128]{0,1:T(8,128)} %copy-done.15) | copy-start | bytes 2359300
  877.8 67.3 %copy-start.21 = (f32[1536,128]{0,1:T(8,128)S(1)}, f32[1536,128]{0,1:T(8,128)}, u32[]{:S(2)}) copy-start(f32[1536,128]{0,1:T(8,128)} %copy-done.20) | copy-start | bytes 2359300
  962.0 216.9 %all-reduce.20.cloned.1.call-start = ((), (), s32[]{:S(2)}) async-start(), calls=%async_computation.6 | async-start | bytes 2097152 | tf_op jit(solution)/shard_map/psum | solution.py:18
  1090.3 347.9 %all-reduce.14.cloned.1.call-start = ((), (), s32[]{:S(2)}) async-start(), calls=%async_computation.3 | async-start | bytes 3145728 | tf_op jit(solution)/shard_map/psum | solution.py:18
  1184.4 68.5 %copy-start.30 = (f32[512,512]{1,0:T(8,128)}, f32[512,512]{1,0:T(8,128)S(1)}, u32[]{:S(2)}) copy-start(f32[512,512]{1,0:T(8,128)S(1)} %fusion.31) | copy-start | bytes 3145732
  1218.5 102.9 %copy-start.23 = (f32[1536,128]{1,0:T(8,128)S(1)}, f32[1536,128]{1,0:T(8,128)}, u32[]{:S(2)}) copy-start(f32[1536,128]{1,0:T(8,128)} %get-tuple-element.44) | copy-start | bytes 2359300
  1253.1 69.2 %copy-start.27 = (f32[1536,128]{1,0:T(8,128)S(1)}, f32[1536,128]{1,0:T(8,128)}, u32[]{:S(2)}) copy-start(f32[1536,128]{1,0:T(8,128)} %get-tuple-element.43) | copy-start | bytes 2359300
  1271.0 54.5 %copy-start.26 = (f32[1536,128]{1,0:T(8,128)S(1)}, f32[1536,128]{1,0:T(8,128)}, u32[]{:S(2)}) copy-start(f32[1536,128]{1,0:T(8,128)} %get-tuple-element.42) | copy-start | bytes 2359300
  1322.3 14.0 copy-start.3
  1325.5 10.8 copy-start.9
  1371.2 67.4 %copy-start.4 = (f32[128,1536]{1,0:T(8,128)S(1)}, f32[128,1536]{1,0:T(8,128)}, u32[]{:S(2)}) copy-start(f32[128,1536]{1,0:T(8,128)} %copy-done.3) | copy-start | bytes 2359300
  1371.2 67.4 %copy-start.10 = (f32[1536,128]{0,1:T(8,128)S(1)}, f32[1536,128]{0,1:T(8,128)}, u32[]{:S(2)}) copy-start(f32[1536,128]{0,1:T(8,128)} %copy-done.9) | copy-start | bytes 2359300
  1371.2 67.4 %copy-start.14 = (f32[1536,128]{0,1:T(8,128)S(1)}, f32[1536,128]{0,1:T(8,128)}, u32[]{:S(2)}) copy-start(f32[1536,128]{0,1:T(8,128)} %copy-done.13) | copy-start | bytes 2359300
  1371.2 67.5 %copy-start.19 = (f32[1536,128]{0,1:T(8,128)S(1)}, f32[1536,128]{0,1:T(8,128)}, u32[]{:S(2)}) copy-start(f32[1536,128]{0,1:T(8,128)} %copy-done.18) | copy-start | bytes 2359300
  1438.7 13.6 copy-start.1
  (10 other events, 39.6 us)
Sparse Core Ops, SparseCore 0:
  466.3 128.0 all-reduce.17
  597.2 88.4 all-reduce.21
  856.1 88.4 all-reduce.11
  962.1 125.5 all-reduce.15
  1090.4 88.4 all-reduce.19
  1349.7 88.3 all-reduce.13
where the time goes:
time: 1470 us; the launch traced here: 1460 us
  waiting for transfers between devices  859 us (58%)
  other arithmetic  273 us (19%)
  matrix products  160 us (11%)
  local copies, waits for them, and re-layouts  133 us (9%)
  between operations  20 us (1%)
    psum x6, waiting for transfers between devices, broadcast(): return lax.psum(jnp.where(mine, shard, jnp.zeros_like(shard)), axis)  548 us
    all_to_all x1, waiting for transfers between devices, per_device(): lax.all_to_all(outgoing, 'pcol', split_axis=0, concat_axis=0, tiled=True)  263 us
    another operation x29, other arithmetic, per_device(): factor = jnp.linalg.cholesky(pivot_block)  158 us
    another operation x7, other arithmetic, per_device(): lax.linalg.triangular_solve(factor, panel_rows, left_side=False, lower=Tr...  82.2 us
    dot_general x1, matrix products, per_device(): jnp.einsum('chnl,bchnxy->clbxy', row_place, incoming, precision=HIGHEST)  55.5 us
    all_to_all x1, waiting for transfers between devices, per_device(): lax.all_to_all(rows_sorted.reshape(row_procs, row_send * BLOCK, col_block...  48.5 us
    dot_general x1, matrix products, per_device(): jnp.einsum('cbs,clbxy->lxsy', col_place, gathered_rows, precision=HIGHEST)  33.7 us
    another operation x14, matrix products, per_device(): lax.linalg.triangular_solve(factor, panel_rows, left_side=False, lower=Tr...  29.5 us
  transfers between devices with their start and end apart: 8, of which 8 were waited for; matrix products, arithmetic and copies ran while one was open for 5% of the time, Pallas kernels for 0%

commit v1 on v0

v1 whole, which is shorter than its diff:
```python
import functools

import jax
import jax.numpy as jnp
from jax import lax
from jax.experimental import pallas as pl
from jax.experimental.pallas import tpu as pltpu
from jax.sharding import PartitionSpec as P

BLOCK = 128
HEAD = 8
F32 = jnp.float32
BF16 = jnp.bfloat16
HIGHEST = lax.Precision.HIGHEST
MIB = 1024 * 1024

PLANE_GROUPS = [[16 * p + 4 * x + w for w in range(4) for p in range(8)] for x in range(4)]


def pack_rows(child, child_map):
    def kernel(map_ref, child_ref, out_ref, buf, turned, sems):
        c = lax.axis_index("prow") // 4
        shift = map_ref[c * 64] % 16

        def fetch(i):
            rows = pl.ds(pl.multiple_of(i * BLOCK, BLOCK), BLOCK)
            return pltpu.make_async_copy(child_ref.at[rows], buf.at[i], sems.at[0, i])

        def store(i):
            residue = (i + shift) % 16
            return pltpu.make_async_copy(
                turned.at[i], out_ref.at[:, residue % 8, residue // 8], sems.at[1, i]
            )

        def forward(i):
            fetch(i).wait()
            for w in range(4):
                b = (w - shift + 16) % 4
                turned[i, w] = buf[i, :, pl.ds(pl.multiple_of(b * BLOCK, BLOCK), BLOCK)]
            store(i).start()

        pl.loop(0, 16)(lambda i: fetch(i).start())
        pl.loop(0, 16)(forward)
        pl.loop(0, 16)(lambda i: store(i).wait())

    return pl.pallas_call(
        kernel,
        out_shape=jax.ShapeDtypeStruct((4, 8, 2, BLOCK, BLOCK), F32),
        in_specs=[pl.BlockSpec(memory_space=pltpu.SMEM), pl.BlockSpec(memory_space=pl.ANY)],
        out_specs=pl.BlockSpec(memory_space=pl.ANY),
        scratch_shapes=[
            pltpu.VMEM((16, BLOCK, 4 * BLOCK), F32),
            pltpu.VMEM((16, 4, BLOCK, BLOCK), F32),
            pltpu.SemaphoreType.DMA((2, 16)),
        ],
        compiler_params=pltpu.CompilerParams(vmem_limit_bytes=16 * MIB),
        cost_estimate=pl.CostEstimate(flops=0, bytes_accessed=8 * MIB, transcendentals=0),
        name="pack_rows",
    )(child_map, child)


def pack_cols(arrived, child_map):
    def kernel(map_ref, in_ref, *refs):
        out_refs, (buf, sems) = refs[:4], refs[4:]
        q = lax.axis_index("pcol")
        x, w = q // 4, q % 4

        def fetch(k):
            d, c = k // 2, k % 2
            column = 4 * ((x + d) % 4) + w
            a = ((column - map_ref[c * 64] % 16 + 16) % 16) // 4
            return pltpu.make_async_copy(in_ref.at[a, c], buf.at[k], sems.at[0, k])

        def store(k):
            return pltpu.make_async_copy(buf.at[k], out_refs[k // 2].at[k % 2], sems.at[1, k])

        for k in range(8):
            fetch(k).start()
        for k in range(8):
            fetch(k).wait()
            store(k).start()
        for k in range(8):
            store(k).wait()

    return pl.pallas_call(
        kernel,
        out_shape=[jax.ShapeDtypeStruct((2, 4, 2, BLOCK, BLOCK), F32)] * 4,
        in_specs=[pl.BlockSpec(memory_space=pltpu.SMEM), pl.BlockSpec(memory_space=pl.ANY)],
        out_specs=[pl.BlockSpec(memory_space=pl.ANY)] * 4,
        scratch_shapes=[
            pltpu.VMEM((8, 4, 2, BLOCK, BLOCK), F32), pltpu.SemaphoreType.DMA((2, 8))
        ],
        compiler_params=pltpu.CompilerParams(vmem_limit_bytes=16 * MIB),
        cost_estimate=pl.CostEstimate(flops=0, bytes_accessed=8 * MIB, transcendentals=0),
        name="pack_cols",
    )(child_map, arrived)


def diag_block(values):
    rows = lax.broadcasted_iota(jnp.int32, (BLOCK, BLOCK), 0)
    cols = lax.broadcasted_iota(jnp.int32, (BLOCK, BLOCK), 1)
    return jnp.where(rows == cols, jnp.broadcast_to(values, (BLOCK, BLOCK)), 0.0)


def local_row(map_ref, c, h, n, p):
    shift = map_ref[c * 64] % 16
    i = (p + 8 * n - shift + 16) % 16
    return map_ref[c * 64 + 16 * h + i] // 8


def local_col(map_ref, c, t, q):
    shift = map_ref[c * 64] % 16
    return map_ref[c * 64 + 16 * t + (q - shift + 16) % 16] // 16


def panel_terms(front, diagonal, arrived, child_map):
    def kernel(map_ref, front_ref, diag_ref, in_ref, *refs):
        out_refs, head_ref, (total, buf, sems) = refs[:4], refs[4], refs[5:]
        p, q = lax.axis_index("prow"), lax.axis_index("pcol")
        x, w = q // 4, q % 4
        chosen, copies = [], []
        for e in range(2):
            for c in range(2):
                at = (4 * e + w - map_ref[c * 64] % 16 + 16) % 16
                chosen.append(map_ref[c * 64 + 16 * x + at] // 16 == 0)
                copies.append(
                    pltpu.make_async_copy(
                        in_ref.at[at // 4, c], buf.at[2 * e + c], sems.at[2 * e + c]
                    )
                )
                copies[-1].start()
        total[...] = jnp.zeros_like(total)

        @pl.when(x < 2)
        def _():
            for l in range(12):
                total[l % 2 * 2 + x, l // 2] = front_ref[l * BLOCK : (l + 1) * BLOCK, :]

        @pl.when(p == q)
        def _():
            total[x, 0] += diag_block(diag_ref[pl.ds(q, 1), :])

        for k in range(4):
            e, c = k // 2, k % 2
            copies[k].wait()

            @pl.when(chosen[k])
            def _():
                def add(i):
                    l = local_row(map_ref, c, i // 2, i % 2, p)
                    total[l % 2 * 2 + e, l // 2] += buf[k, i // 2, i % 2]

                pl.loop(0, 8)(add)

        for d in range(4):
            out_refs[d][...] = total[(x + d) % 4]
        for e in range(2):
            head_ref[e] = total[e, 0]

    return pl.pallas_call(
        kernel,
        out_shape=[jax.ShapeDtypeStruct((6, BLOCK, BLOCK), F32)] * 4
        + [jax.ShapeDtypeStruct((2, BLOCK, BLOCK), F32)],
        grid=(1,),
        in_specs=[
            pl.BlockSpec(memory_space=pltpu.SMEM),
            pl.BlockSpec((12 * BLOCK, BLOCK), lambda i: (0, 0)),
            pl.BlockSpec((96, BLOCK), lambda i: (0, 0)),
            pl.BlockSpec(memory_space=pl.ANY),
        ],
        out_specs=[pl.BlockSpec((6, BLOCK, BLOCK), lambda i: (0, 0, 0))] * 4
        + [pl.BlockSpec((2, BLOCK, BLOCK), lambda i: (0, 0, 0))],
        scratch_shapes=[
            pltpu.VMEM((4, 6, BLOCK, BLOCK), F32),
            pltpu.VMEM((4, 4, 2, BLOCK, BLOCK), F32),
            pltpu.SemaphoreType.DMA((4,)),
        ],
        compiler_params=pltpu.CompilerParams(vmem_limit_bytes=24 * MIB),
        cost_estimate=pl.CostEstimate(flops=0, bytes_accessed=5 * MIB, transcendentals=0),
        name="panel_terms",
    )(child_map, front, diagonal, arrived)


NN = ((1,), (0,))
NT = ((1,), (1,))
TN = ((0,), (0,))


def dot(a, b, contract):
    dims = (contract, ((), ()))
    return lax.dot_general(a, b, dims, precision=HIGHEST, preferred_element_type=F32)


def dot1(a, b, contract):
    return lax.dot_general(a, b, (contract, ((), ())), preferred_element_type=F32)


def split(value):
    high = value.astype(BF16)
    return high, (value - high.astype(F32)).astype(BF16)


def dot3(a, b, contract):
    (ah, al), (bh, bl) = a, b
    return dot1(ah, bl, contract) + dot1(al, bh, contract) + dot1(ah, bh, contract)


def square_iotas(size):
    shape = (size, size)
    return lax.broadcasted_iota(jnp.int32, shape, 0), lax.broadcasted_iota(jnp.int32, shape, 1)


def newton_factor(a_ref, x_ref):
    ri, ci = square_iotas(a_ref.shape[0])
    one = jnp.where(ri == ci, 1.0, 0.0)

    def lower_half(e):
        return jnp.where(ri > ci, e, jnp.where(ri == ci, 0.5 * e, 0.0))

    a = a_ref[...]
    pivots = jnp.where(ri == ci, a, 0.0)
    scale = lax.rsqrt(jnp.sum(pivots, axis=0, keepdims=True))
    f = split(jnp.where(ri > ci, a * lax.rsqrt(jnp.sum(pivots, axis=1, keepdims=True)) * scale, 0.0))
    x = (one - (f[0].astype(F32) + f[1].astype(F32)) + dot1(f[0], f[0], NN)) * scale
    xs = split(x)
    e = dot3(split(dot3(xs, split(a), NN)), xs, NT) - one
    f = split(lower_half(e))
    g = dot3(f, xs, NN)
    x = x - g + dot1(f[0], g.astype(BF16), NN)
    t = dot(x, a, NN)
    e = dot(t, x, NT) - one
    f = split(lower_half(e))
    x_ref[...] = x - dot3(f, split(x), NN)
    a_ref[...] = jnp.where(ci >= ri, t - dot3(f, split(t), NN), 0.0)
    return jnp.max(jnp.sum(jnp.abs(e), axis=1, keepdims=True))


def direct_factor(t_ref):
    size = t_ref.shape[0]
    ri, ci = square_iotas(size)
    lane = lax.broadcasted_iota(jnp.int32, (1, 2 * size), 1)
    down = lax.broadcasted_iota(jnp.int32, (size, 1), 0)

    def step(j):
        row = t_ref[pl.ds(j, 1), :]
        row = row * lax.rsqrt(jnp.sum(jnp.where(lane == j, row, 0.0), axis=1, keepdims=True))
        col = jnp.broadcast_to(row[:, :size], (size, size))
        col = jnp.sum(jnp.where(ri == ci, col, 0.0), axis=1, keepdims=True)
        t_ref[...] = t_ref[...] - jnp.where(down > j, col, 0.0) * row
        t_ref[pl.ds(j, 1), :] = row

    pl.loop(0, size)(step)


def head_factor(gathered):
    size, wide = HEAD * BLOCK, 2 * BLOCK

    def kernel(*refs):
        in_refs, (wh_ref, wl_ref, own_ref), scratch = refs[:8], refs[8:11], refs[11:]
        m_ref, u_ref, w_ref, a_ref, x_ref, t_ref = scratch
        p, q = lax.axis_index("prow"), lax.axis_index("pcol")

        def place(k, in_ref, core_back, z_back):
            core = (q + core_back) % 2
            y = (2 * (p // 4) + (q // 2) % 2 - k // 2 + 4) % 4
            z = (p - z_back + 4) % 4
            row, col = y // 2 * 4 + z, k % 2 * 4 + y % 2 * 2 + core
            rows = pl.ds(pl.multiple_of(row * BLOCK, BLOCK), BLOCK)
            cols = pl.ds(pl.multiple_of(col * BLOCK, BLOCK), BLOCK)
            m_ref[rows, cols] = in_ref[k]

        for at in range(8):
            pl.loop(0, 8)(
                functools.partial(place, in_ref=in_refs[at], core_back=at // 4, z_back=at % 4)
            )
        for i in range(HEAD):
            for j in range(i, HEAD):
                rows, cols = slice(i * BLOCK, (i + 1) * BLOCK), slice(j * BLOCK, (j + 1) * BLOCK)
                value = m_ref[cols, rows].T
                if i // 4 == j // 4:
                    value = 0.5 * (m_ref[rows, cols] + value)
                u_ref[rows, cols] = value
                if i // 2 == j // 2 and i != j:
                    u_ref[cols, rows] = value.T
        ri, ci = square_iotas(wide)
        for s in range(0, size, wide):
            e = s + wide
            a_ref[...] = u_ref[s:e, s:e]
            off = newton_factor(a_ref, x_ref)

            @pl.when(jnp.logical_not(off < 5e-4))
            def _():
                t_ref[:, :wide] = u_ref[s:e, s:e]
                t_ref[:, wide:] = jnp.where(ri == ci, 1.0, 0.0)
                direct_factor(t_ref)
                a_ref[...] = jnp.where(ci >= ri, t_ref[:, :wide], 0.0)
                x_ref[...] = jnp.where(ri >= ci, t_ref[:, wide:], 0.0)

            u_ref[s:e, s:e] = a_ref[...]
            w_ref[s:e, s:e] = x_ref[...]
            inverse = split(x_ref[...])
            if s:
                w_ref[s:e, 0:s] = dot3(inverse, split(w_ref[s:e, 0:s]), NN)
            done = split(w_ref[s:e, 0:e])
            wh_ref[s:e, 0:e], wl_ref[s:e, 0:e] = done
            if e < size:
                wh_ref[s:e, e:] = jnp.zeros((wide, size - e), BF16)
                wl_ref[s:e, e:] = jnp.zeros((wide, size - e), BF16)
                right = dot3(inverse, split(u_ref[s:e, e:]), NN)
                u_ref[s:e, e:] = right
                right = split(right)
                for j in range(e, size, wide):
                    left = tuple(v[:, j - e : j - e + wide] for v in right)
                    rest = tuple(v[:, j - e :] for v in right)
                    u_ref[j : j + wide, j:] = u_ref[j : j + wide, j:] - dot3(left, rest, TN)
                    change = dot3(left, done, TN)
                    if s:
                        w_ref[j : j + wide, 0:s] = w_ref[j : j + wide, 0:s] - change[:, 0:s]
                    w_ref[j : j + wide, s:e] = -change[:, s:e]
        own_ref[...] = jnp.zeros((BLOCK, BLOCK), F32)

        @pl.when(q <= p)
        def _():
            rows = pl.ds(pl.multiple_of(q * BLOCK, BLOCK), BLOCK)
            cols = pl.ds(pl.multiple_of(p * BLOCK, BLOCK), BLOCK)
            own_ref[...] = u_ref[rows, cols].T

    vmem = pl.BlockSpec(memory_space=pltpu.VMEM)
    square = pltpu.VMEM((size, size), F32)
    return pl.pallas_call(
        kernel,
        out_shape=[
            jax.ShapeDtypeStruct((size, size), BF16),
            jax.ShapeDtypeStruct((size, size), BF16),
            jax.ShapeDtypeStruct((BLOCK, BLOCK), F32),
        ],
        in_specs=[vmem] * 8,
        out_specs=[vmem] * 3,
        scratch_shapes=[square] * 3
        + [pltpu.VMEM((wide, wide), F32)] * 2
        + [pltpu.VMEM((wide, 2 * wide), F32)],
        compiler_params=pltpu.CompilerParams(vmem_limit_bytes=40 * MIB),
        cost_estimate=pl.CostEstimate(
            flops=20_000_000_000, bytes_accessed=8 * MIB, transcendentals=0
        ),
        name="head_factor",
    )(*gathered)


def solve_columns(col_panel, inverse):
    size, wide = HEAD * BLOCK, 6 * BLOCK

    def kernel(wh, wl, in0, in1, in2, in3, oh_ref, ol_ref, ch, cl, yh, yl):
        p, q = lax.axis_index("prow"), lax.axis_index("pcol")
        for z_back, in_ref in enumerate((in0, in1, in2, in3)):
            for y_back in range(2):
                m = (p // 4 + y_back) % 2 * 4 + (p + 4 - z_back) % 4
                cols = pl.ds(pl.multiple_of(m * BLOCK, BLOCK), BLOCK)
                for s in range(6):
                    rows = slice(s * BLOCK, (s + 1) * BLOCK)
                    ch[rows, cols], cl[rows, cols] = split(in_ref[y_back, s])
        for i in range(0, size, 256):
            e = i + 256
            y = dot3((ch[:, 0:e], cl[:, 0:e]), (wh[i:e, 0:e], wl[i:e, 0:e]), NT)
            yh[:, i:e], yl[:, i:e] = split(y)
        for i in range(0, size, 256):
            e = i + 256
            z = dot3((yh[:, i:], yl[:, i:]), (wh[i:, i:e], wl[i:, i:e]), NN)
            oh_ref[:, i:e], ol_ref[:, i:e] = split(z)

        @pl.when(q < HEAD)
        def _():
            rows = pl.ds(pl.multiple_of(q * BLOCK, BLOCK), BLOCK)
            oh_ref[0:BLOCK, :] = -wh[rows, :]
            ol_ref[0:BLOCK, :] = -wl[rows, :]

    vmem = pl.BlockSpec(memory_space=pltpu.VMEM)
    return pl.pallas_call(
        kernel,
        out_shape=[jax.ShapeDtypeStruct((wide, size), BF16)] * 2,
        in_specs=[vmem] * 6,
        out_specs=[vmem] * 2,
        scratch_shapes=[pltpu.VMEM((wide, size), BF16)] * 4,
        compiler_params=pltpu.CompilerParams(vmem_limit_bytes=32 * MIB),
        cost_estimate=pl.CostEstimate(
            flops=8_000_000_000, bytes_accessed=10 * MIB, transcendentals=0
        ),
        name="solve_columns",
    )(*inverse, *col_panel)


def finish(front, diagonal, arrived, row_panel, solved, own, child_map):
    size, group, wide = HEAD * BLOCK, 4, 6 * BLOCK

    def kernel(
        map_ref, sh, sl, own_ref, diag_ref, in0, in1, in2, in3, row_ref, front_ref, out_ref
    ):
        step = pl.program_id(0)
        p, q = lax.axis_index("prow"), lax.axis_index("pcol")
        out_ref[...] = front_ref[...]
        for s in range(6):
            l = 2 * s + jnp.where(q >= 8, 1, 0)

            @pl.when((q % 8 == p) & (l // group == step))
            def _():
                rows = pl.ds(pl.multiple_of((l % group) * BLOCK, BLOCK), BLOCK)
                out_ref[rows, s * BLOCK : (s + 1) * BLOCK] += diag_block(
                    diag_ref[pl.ds(16 * s + q, 1), :]
                )

        def add(k, in_ref, t):
            c, h, n = k // 8, (k // 2) % 4, k % 2
            l = local_row(map_ref, c, h, n, p)
            s = local_col(map_ref, c, t, q)

            @pl.when(l // group == step)
            def _():
                rows = pl.ds(pl.multiple_of((l % group) * BLOCK, BLOCK), BLOCK)
                cols = pl.ds(pl.multiple_of(s * BLOCK, BLOCK), BLOCK)
                out_ref[rows, cols] += in_ref[c, h, n]

        for d, in_ref in enumerate((in0, in1, in2, in3)):
            pl.loop(0, 16)(functools.partial(add, in_ref=in_ref, t=(q // 4 + 4 - d) % 4))

        @pl.when(q < HEAD)
        def _():
            out_ref[:, 0:BLOCK] = jnp.zeros((group * BLOCK, BLOCK), F32)

        rows = []
        for k in range(group):
            rows.append(
                jnp.concatenate([row_ref[k % 2 * 8 + m, k // 2] for m in range(HEAD)], axis=1)
            )
        rows = split(jnp.concatenate(rows, axis=0))
        for j in range(0, wide, 256):
            e = j + 256
            out_ref[:, j:e] -= dot3(rows, (sh[j:e, :], sl[j:e, :]), NT)

        @pl.when(step == 0)
        def _():
            out_ref[0:BLOCK, :] = jnp.zeros((BLOCK, wide), F32)
            out_ref[0:BLOCK, 0:BLOCK] = own_ref[...]

    def whole(*shape):
        return pl.BlockSpec(shape, lambda i: (0,) * len(shape), pipeline_mode=pl.Buffered(1))

    return pl.pallas_call(
        kernel,
        out_shape=jax.ShapeDtypeStruct((12 * BLOCK, wide), F32),
        grid=(12 // group,),
        in_specs=[
            pl.BlockSpec(memory_space=pltpu.SMEM),
            whole(wide, size),
            whole(wide, size),
            whole(BLOCK, BLOCK),
            whole(96, BLOCK),
            *[whole(2, 4, 2, BLOCK, BLOCK)] * 4,
            pl.BlockSpec((16, group // 2, BLOCK, BLOCK), lambda i: (0, i, 0, 0)),
            pl.BlockSpec((group * BLOCK, wide), lambda i: (i, 0)),
        ],
        out_specs=pl.BlockSpec((group * BLOCK, wide), lambda i: (i, 0)),
        compiler_params=pltpu.CompilerParams(vmem_limit_bytes=60 * MIB),
        cost_estimate=pl.CostEstimate(
            flops=8_000_000_000, bytes_accessed=24 * MIB, transcendentals=0
        ),
        name="finish",
    )(child_map, *solved, own, diagonal, *arrived, row_panel, front)


def ahead_x(d):
    return [(4 * x + w, 4 * ((x + d) % 4) + w) for x in range(4) for w in range(4)]


def ahead_z(d):
    return [(4 * h + z, 4 * h + (z + d) % 4) for h in range(2) for z in range(4)]


def ahead_y(d):
    def rank(y, z, x, core):
        return (4 * (y // 2) + z) * 16 + 4 * x + 2 * (y % 2) + core

    return [
        (rank(y, z, x, core), rank((y + d) % 4, z, x, core))
        for y in range(4) for z in range(4) for x in range(4) for core in range(2)
    ]


OTHER_CORE = [(k, k ^ 1) for k in range(16)]
BOTH = ("prow", "pcol")


def gather_head(terms):
    held = terms
    for d in (1, 2, 3):
        held = held + lax.ppermute(terms, "pcol", ahead_x(d))
    summed = held
    along_y = [held] + [lax.ppermute(held, BOTH, ahead_y(d)) for d in (1, 2, 3)]
    held = jnp.concatenate(along_y, axis=0)
    along_z = [held] + [lax.ppermute(held, "prow", ahead_z(d)) for d in (1, 2, 3)]
    return summed, along_z, [lax.ppermute(part, "pcol", OTHER_CORE) for part in along_z]


def gather_columns(piece):
    turned = lax.ppermute(
        piece,
        BOTH,
        [
            (p * 16 + (2 * par + e) * 4 + w, (4 * e + w) * 16 + p + 8 * par)
            for p in range(8) for par in range(2) for e in range(2) for w in range(4)
        ],
    )
    other = lax.ppermute(turned, "prow", [(p, p ^ 4) for p in range(8)])
    held = jnp.stack([turned, other], axis=0)
    return [held] + [lax.ppermute(held, "prow", ahead_z(d)) for d in (1, 2, 3)]


def per_device(front, diagonal, child, child_map):
    child_map = child_map.reshape(128)
    diagonal = diagonal.reshape(96, BLOCK)
    sent = pack_rows(child, child_map).reshape(64, BLOCK, BLOCK)
    sent = lax.all_to_all(sent, BOTH, 0, 0, axis_index_groups=PLANE_GROUPS, tiled=True)
    sent = sent.reshape(4, 2, 4, 2, BLOCK, BLOCK)
    *terms, head_terms = panel_terms(front, diagonal, sent, child_map)
    summed, along_z, twins = gather_head(head_terms)
    summed, *terms = lax.optimization_barrier([summed, *terms])
    behind = [lax.ppermute(terms[d], "pcol", ahead_x(d)) for d in (1, 2, 3)]
    *behind, last = lax.optimization_barrier([*behind, along_z[3]])
    piece = terms[0] + behind[0] + behind[1] + behind[2]
    gathered = along_z[:3] + [last] + twins
    blocks = pack_cols(sent, child_map)
    piece, *ahead = lax.optimization_barrier([piece, *blocks[1:]])
    arrived = [blocks[0]]
    for d in (1, 2, 3):
        arrived.append(lax.ppermute(ahead[d - 1], "pcol", ahead_x(d)))
    row_panel = lax.all_gather(piece, "pcol")
    col_panel = gather_columns(piece)
    *inverse, own = head_factor(gathered)
    solved = solve_columns(col_panel, inverse)
    return finish(front, diagonal, arrived, row_panel, solved, own, child_map)


def solution(mesh):
    return jax.shard_map(
        per_device,
        mesh=mesh,
        in_specs=(P("prow", "pcol"), P(), P("prow", "pcol"), P()),
        out_specs=P("prow", "pcol"),
        check_vma=False,
    )
```

time: 1470 us -> 428 us (0.29)
  the two profiles are of different devices: /device:TPU:0 before, /device:TPU:40 now
where the time goes in v1:
time: 428 us; the launch traced here: 427 us
  Pallas kernels  219 us (51%)
  starting transfers between devices  68.4 us (16%)
  waiting for transfers between devices  59.3 us (14%)
  blocking collectives  56.4 us (13%)
  between operations  13.6 us (3%)
  local copies, waits for them, and re-layouts  9.26 us (2%)
    pallas_call x1, Pallas kernels, head_factor(): pl.pallas_call(kernel, out_shape=[jax.ShapeDtypeStruct((size, size), BF16...  182 us
    all_to_all x1, blocking collectives, per_device(): lax.all_to_all(sent, BOTH, 0, 0, axis_index_groups=PLANE_GROUPS, tiled=True)  56.4 us
    ppermute x3, starting transfers between devices, gather_columns(): return [held] + [lax.ppermute(held, 'prow', ahead_z(d)) for d in (1, 2, 3)]  26.8 us
    pallas_call x1, Pallas kernels, finish(): pl.pallas_call(kernel, out_shape=jax.ShapeDtypeStruct((12 * BLOCK, wide),...  24 us
    ppermute x3, waiting for transfers between devices, per_device(): behind = [lax.ppermute(terms[d], 'pcol', ahead_x(d)) for d in (1, 2, 3)]  13.6 us
    ppermute x1, waiting for transfers between devices, gather_columns(): lax.ppermute(piece, BOTH, [(p * 16 + (2 * par + e) * 4 + w, (4 * e + w) *...  12.4 us
    ppermute x3, waiting for transfers between devices, gather_columns(): return [held] + [lax.ppermute(held, 'prow', ahead_z(d)) for d in (1, 2, 3)]  11.6 us
    ppermute x1, starting transfers between devices, gather_columns(): other = lax.ppermute(turned, 'prow', [(p, p ^ 4) for p in range(8)])  10.5 us
  transfers between devices with their start and end apart: 25, of which 11 were waited for; matrix products, arithmetic and copies ran while one was open for 0% of the time, Pallas kernels for 45%

profile of v1, /device:TPU:40, one launch (start us, length us, event | category | flops | bytes accessed | tf_op | source)
XLA Modules:
  0.0 427.1 jit_solution(14574126920169006177)
XLA Ops:
  7.3 2.2 copy-done
  9.5 2.5 pack_rows.1
  12.0 56.4 %all_to_all.5 = f32[64,128,128]{2,1,0:T(8,128)S(1)} all-to-all(f32[64,128,128]{2,1,0:T(8,128)S(1)} %bitcast.8), channel_id=1, replica_groups={{0,16,32,48,64,80,96,112,1,17,33,49,65,81,97,113,2,18,34,50,66,82,98,11..., dimensions={0} | all-to-all | bytes 8388608 | tf_op jit(solution)/shard_map/all_to_all | solution.py:521
  68.4 1.4 panel_terms.1
  69.8 1.8 collective-permute-start
  71.7 2.1 collective-permute-start.1
  73.8 1.4 collective-permute-start.2
  75.2 1.8 collective-permute-done
  77.0 3.9 collective-permute-done.1
  81.4 3.3 collective-permute-start.4
  84.7 2.6 collective-permute-done.3
  87.3 2.0 collective-permute-done.4
  89.3 1.6 collective-permute-done.5
  91.2 2.5 collective-permute-start.10
  93.7 2.1 collective-permute-start.9
  95.8 1.4 pack_cols.1
  99.2 10.3 %collective-permute-done.10 = f32[6,128,128]{2,1,0:T(8,128)S(1)} collective-permute-done((f32[6,128,128]{2,1,0:T(8,128)S(1)}, f32[6,128,128]{2,1,0:T(8,128)S(1)}, u32[]{:S(2)}, u32[]{:S(2)}) %collective-permute-start.10) | collective-permute-done | bytes 393248 | tf_op jit(solution)/shard_map/ppermute | solution.py:526
  109.4 3.4 collective-permute-done.8
  113.7 1.9 collective-permute-start.16
  115.6 12.4 %collective-permute-done.16 = f32[6,128,128]{2,1,0:T(8,128)S(1)} collective-permute-done((f32[6,128,128]{2,1,0:T(8,128)}, f32[6,128,128]{2,1,0:T(8,128)S(1)}, u32[]{:S(2)}, u32[]{:S(2)}) %collective-permute-start.16) | collective-permute-done | bytes 393248 | tf_op jit(solution)/shard_map/ppermute | solution.py:504
  128.0 10.5 %collective-permute-start.17 = (f32[6,128,128]{2,1,0:T(8,128)S(1)}, f32[6,128,128]{2,1,0:T(8,128)S(1)}, u32[]{:S(2)}, u32[]{:S(2)}) collective-permute-start(f32[6,128,128]{2,1,0:T(8,128)S(1)} %collective-permute-done.16), channel_id=1, source_target_pairs={{0,64},{16,80},{32,96},{48,112},{64,0},{80,16},{96,32},{112,48},{1... | collective-permute-start | bytes 1179656 | tf_op jit(solution)/shard_map/ppermute | solution.py:512
  138.5 3.5 collective-permute-start.6
  142.0 5.5 %collective-permute-start.7 = (f32[8,128,128]{2,1,0:T(8,128)S(1)}, f32[8,128,128]{2,1,0:T(8,128)S(1)}, u32[]{:S(2)}, u32[]{:S(2)}) collective-permute-start(f32[8,128,128]{2,1,0:T(8,128)S(1)} %pad_maximum_fusion.1.refs_0_), channel_id=1, source_target_pairs={{0,32},{16,48},{32,0},{48,16},{64,96},{80,112},{96,64},{112,80},{1... | collective-permute-start | bytes 1572872 | tf_op jit(solution)/shard_map/ppermute | solution.py:499
  147.5 8.8 %collective-permute-done.17 = f32[6,128,128]{2,1,0:T(8,128)S(1)} collective-permute-done((f32[6,128,128]{2,1,0:T(8,128)S(1)}, f32[6,128,128]{2,1,0:T(8,128)S(1)}, u32[]{:S(2)}, u32[]{:S(2)}) %collective-permute-start.17) | collective-permute-done | bytes 393248 | tf_op jit(solution)/shard_map/ppermute | solution.py:512
  156.4 2.1 collective-permute-start.18
  162.8 2.9 collective-permute-start.23
  165.7 9.1 %collective-permute-start.19 = (f32[2,6,128,128]{3,2,1,0:T(8,128)S(1)}, f32[2,6,128,128]{3,2,1,0:T(8,128)S(1)}, u32[]{:S(2)}, u32[]{:S(2)}) collective-permute-start(f32[2,6,128,128]{3,2,1,0:T(8,128)S(1)} %pad_maximum_fusion.in0), channel_id=1, source_target_pairs={{0,32},{16,48},{32,0},{48,16},{64,96},{80,112},{96,64},{112,80},{1... | collective-permute-start | bytes 2359304 | tf_op jit(solution)/shard_map/ppermute | solution.py:514
  174.8 11.6 %collective-permute-done.18.in1 = f32[2,6,128,128]{3,2,1,0:T(8,128)S(1)} collective-permute-done((f32[2,6,128,128]{3,2,1,0:T(8,128)S(1)}, f32[2,6,128,128]{3,2,1,0:T(8,128)S(1)}, u32[]{:S(2)}, u32[]{:S(2)}) %collective-permute-start.18) | collective-permute-done | bytes 786464 | tf_op jit(solution)/shard_map/ppermute | solution.py:514
  186.4 15.5 %collective-permute-start.20 = (f32[2,6,128,128]{3,2,1,0:T(8,128)S(1)}, f32[2,6,128,128]{3,2,1,0:T(8,128)S(1)}, u32[]{:S(2)}, u32[]{:S(2)}) collective-permute-start(f32[2,6,128,128]{3,2,1,0:T(8,128)S(1)} %pad_maximum_fusion.in0), channel_id=1, source_target_pairs={{0,48},{16,0},{32,16},{48,32},{64,112},{80,64},{96,80},{112,96},{1... | collective-permute-start | bytes 2359304 | tf_op jit(solution)/shard_map/ppermute | solution.py:514
  201.9 182.1 %head_factor.1 = (bf16[1024,1024]{1,0:T(8,128)(2,1)S(1)}, bf16[1024,1024]{1,0:T(8,128)(2,1)S(1)}, f32[128,128]{1,0:T(8,128)S(1)}) custom-call(f32[8,128,128]{2,1,0:T(8,128)S(1)} %pad_maximum_fusion.1.refs_0_, f32[8,128,128]{2,1,0:T(8,128)S(1)} %collective-permute-done.6.refs_1_, f32[8,128,128]{2,1,0:T(8,128)S(1)} %collective-permute-done.7.refs_2_, ...), custom_call_target="tpu_custom_call" | custom-call | flops 20000000000 | bytes 8388608 | tf_op jit(solution)/shard_map/head_factor/pallas_call | solution.py:330
  384.1 7.7 %solve_columns.1 = (bf16[768,1024]{1,0:T(8,128)(2,1)S(1)}, bf16[768,1024]{1,0:T(8,128)(2,1)S(1)}) custom-call(bf16[1024,1024]{1,0:T(8,128)(2,1)S(1)} %get-tuple-element.40.wh, bf16[1024,1024]{1,0:T(8,128)(2,1)S(1)} %get-tuple-element.41.wl, f32[2,6,128,128]{3,2,1,0:T(8,128)S(1)} %pad_maximum_fusion.in0, f32[2,6,128,128]{3,2,1,0:T(8,128)S(1)} %collective-permute-done.18.in1, ...), custom_call_target="tpu_custom_call" | custom-call | flops 8000000000 | bytes 10485760 | tf_op jit(solution)/shard_map/solve_columns/pallas_call | solution.py:378
  396.2 24.0 %finish.1 = f32[1536,768]{1,0:T(8,128)} custom-call(s32[128]{0:T(128)} %copy-done.2, bf16[768,1024]{1,0:T(8,128)(2,1)} %copy-done.5, bf16[768,1024]{1,0:T(8,128)(2,1)} %copy-done.6, f32[128,128]{1,0:T(8,128)} %copy-done.7, f32[96,128]{1,0:T(8,128)} %bitcast.11, f32[2,4,2,128,128]{4,3,2,1,0:T(8,128)} %copy-done.3, f32[2,4,2,128,128]{4,3,2,1,0:T(8,128)} %copy-done.8, ...), custom_call_target="tpu_custom_call" | custom-call | flops 8000000000 | bytes 25165824 | tf_op jit(solution)/shard_map/finish/pallas_call | solution.py:447
  (56 shorter events, 13.0 us)
Async XLA Ops:
  6.5 389.7 %all-gather.3.cloned.1.call-start = ((), (), s32[]{:S(2)}) async-start(), calls=%async_computation.1 | async-start | bytes 6684672 | tf_op jit(solution)/shard_map/all_gather | solution.py:535
  7.3 2.2 copy-start
  9.5 86.3 %copy-start.2 = (s32[128]{0:T(128)}, s32[128]{0:T(128)S(1)}, u32[]{:S(2)}) copy-start(s32[128]{0:T(128)S(1)} %reshape.12.map_ref) | copy-start | bytes 1540
  9.5 58.9 %slice-start = ((s8[4718592]{0:T(1024)(128)(4,1)}), s8[4194304]{0:T(1024)(128)(4,1)S(1)}, s32[]{:S(2)}) async-start(s8[4718592]{0:T(1024)(128)(4,1)} %bitcast.9), calls=%async_computation.2 | async-start | bytes 8388608
  12.0 56.4 %slice-start.1 = ((s8[4718592]{0:T(1024)(128)(4,1)}), s8[524288]{0:T(1024)(128)(4,1)S(1)}, s32[]{:S(2)}) async-start(s8[4718592]{0:T(1024)(128)(4,1)} %bitcast.9), calls=%async_computation.3 | async-start | bytes 1048576
  12.0 56.4 %copy-start.1 = (f32[12288]{0:T(1024)S(1)}, f32[12288]{0:T(1024)}, u32[]{:S(2)}) copy-start(f32[12288]{0:T(1024)} %param.5) | copy-start | bytes 147460
  69.8 7.1 %collective-permute-start = (f32[2,128,128]{2,1,0:T(8,128)S(1)}, f32[2,128,128]{2,1,0:T(8,128)S(1)}, u32[]{:S(2)}, u32[]{:S(2)}) collective-permute-start(f32[2,128,128]{2,1,0:T(8,128)S(1)} %get-tuple-element.31), channel_id=1, source_target_pairs={{0,4},{1,5},{2,6},{3,7},{4,8},{5,9},{6,10},{7,11},{8,12},{9,13},{1... | collective-permute-start | bytes 393224 | tf_op jit(solution)/shard_map/ppermute | solution.py:495
  71.7 9.2 %collective-permute-start.1 = (f32[2,128,128]{2,1,0:T(8,128)S(1)}, f32[2,128,128]{2,1,0:T(8,128)S(1)}, u32[]{:S(2)}, u32[]{:S(2)}) collective-permute-start(f32[2,128,128]{2,1,0:T(8,128)S(1)} %get-tuple-element.31), channel_id=1, source_target_pairs={{0,8},{1,9},{2,10},{3,11},{4,12},{5,13},{6,14},{7,15},{8,0},{9,1},... | collective-permute-start | bytes 393224 | tf_op jit(solution)/shard_map/ppermute | solution.py:495
  73.8 7.1 %collective-permute-start.2 = (f32[2,128,128]{2,1,0:T(8,128)S(1)}, f32[2,128,128]{2,1,0:T(8,128)S(1)}, u32[]{:S(2)}, u32[]{:S(2)}) collective-permute-start(f32[2,128,128]{2,1,0:T(8,128)S(1)} %get-tuple-element.31), channel_id=1, source_target_pairs={{0,12},{1,13},{2,14},{3,15},{4,0},{5,1},{6,2},{7,3},{8,4},{9,5},{1... | collective-permute-start | bytes 393224 | tf_op jit(solution)/shard_map/ppermute | solution.py:495
  80.9 6.4 %collective-permute-start.3 = (f32[2,128,128]{2,1,0:T(8,128)S(1)}, f32[2,128,128]{2,1,0:T(8,128)S(1)}, u32[]{:S(2)}, u32[]{:S(2)}) collective-permute-start(f32[2,128,128]{2,1,0:T(8,128)S(1)} %add_add_fusion.1), channel_id=1, source_target_pairs={{0,2},{1,3},{4,6},{5,7},{8,10},{9,11},{12,14},{13,15},{16,18},{17,... | collective-permute-start | bytes 393224 | tf_op jit(solution)/shard_map/ppermute | solution.py:497
  81.4 7.9 %collective-permute-start.4 = (f32[2,128,128]{2,1,0:T(8,128)S(1)}, f32[2,128,128]{2,1,0:T(8,128)S(1)}, u32[]{:S(2)}, u32[]{:S(2)}) collective-permute-start(f32[2,128,128]{2,1,0:T(8,128)S(1)} %add_add_fusion.1), channel_id=1, source_target_pairs={{0,64},{1,65},{4,68},{5,69},{8,72},{9,73},{12,76},{13,77},{16,80},... | collective-permute-start | bytes 393224 | tf_op jit(solution)/shard_map/ppermute | solution.py:497
  84.7 6.2 %collective-permute-start.5 = (f32[2,128,128]{2,1,0:T(8,128)S(1)}, f32[2,128,128]{2,1,0:T(8,128)S(1)}, u32[]{:S(2)}, u32[]{:S(2)}) collective-permute-start(f32[2,128,128]{2,1,0:T(8,128)S(1)} %add_add_fusion.1), channel_id=1, source_target_pairs={{0,66},{1,67},{4,70},{5,71},{8,74},{9,75},{12,78},{13,79},{16,82},... | collective-permute-start | bytes 393224 | tf_op jit(solution)/shard_map/ppermute | solution.py:497
  91.0 21.9 %collective-permute-start.11 = (f32[8,128,128]{2,1,0:T(8,128)S(1)}, f32[8,128,128]{2,1,0:T(8,128)S(1)}, u32[]{:S(2)}, u32[]{:S(2)}) collective-permute-start(f32[8,128,128]{2,1,0:T(8,128)S(1)} %pad_maximum_fusion.1.refs_0_), channel_id=1, source_target_pairs={{0,48},{16,0},{32,16},{48,32},{64,112},{80,64},{96,80},{112,96},{1... | collective-permute-start | bytes 1572872 | tf_op jit(solution)/shard_map/ppermute | solution.py:499
  91.2 18.3 %collective-permute-start.10 = (f32[6,128,128]{2,1,0:T(8,128)S(1)}, f32[6,128,128]{2,1,0:T(8,128)S(1)}, u32[]{:S(2)}, u32[]{:S(2)}) collective-permute-start(f32[6,128,128]{2,1,0:T(8,128)S(1)} %get-tuple-element.38), channel_id=1, source_target_pairs={{0,12},{1,13},{2,14},{3,15},{4,0},{5,1},{6,2},{7,3},{8,4},{9,5},{1... | collective-permute-start | bytes 1179656 | tf_op jit(solution)/shard_map/ppermute | solution.py:526
  93.7 19.1 %collective-permute-start.8 = (f32[6,128,128]{2,1,0:T(8,128)S(1)}, f32[6,128,128]{2,1,0:T(8,128)S(1)}, u32[]{:S(2)}, u32[]{:S(2)}) collective-permute-start(f32[6,128,128]{2,1,0:T(8,128)S(1)} %get-tuple-element.36), channel_id=1, source_target_pairs={{0,4},{1,5},{2,6},{3,7},{4,8},{5,9},{6,10},{7,11},{8,12},{9,13},{1... | collective-permute-start | bytes 1179656 | tf_op jit(solution)/shard_map/ppermute | solution.py:526
  93.7 19.1 %collective-permute-start.9 = (f32[6,128,128]{2,1,0:T(8,128)S(1)}, f32[6,128,128]{2,1,0:T(8,128)S(1)}, u32[]{:S(2)}, u32[]{:S(2)}) collective-permute-start(f32[6,128,128]{2,1,0:T(8,128)S(1)} %get-tuple-element.37), channel_id=1, source_target_pairs={{0,8},{1,9},{2,10},{3,11},{4,12},{5,13},{6,14},{7,15},{8,0},{9,1},... | collective-permute-start | bytes 1179656 | tf_op jit(solution)/shard_map/ppermute | solution.py:526
  113.7 14.3 %collective-permute-start.16 = (f32[6,128,128]{2,1,0:T(8,128)}, f32[6,128,128]{2,1,0:T(8,128)S(1)}, u32[]{:S(2)}, u32[]{:S(2)}) collective-permute-start(f32[6,128,128]{2,1,0:T(8,128)} %add_add_fusion), channel_id=1, source_target_pairs={{0,0},{1,16},{2,32},{3,48},{4,64},{5,80},{6,96},{7,112},{8,8},{9,2... | collective-permute-start | bytes 1179656 | tf_op jit(solution)/shard_map/ppermute | solution.py:504
  128.0 28.3 %collective-permute-start.17 = (f32[6,128,128]{2,1,0:T(8,128)S(1)}, f32[6,128,128]{2,1,0:T(8,128)S(1)}, u32[]{:S(2)}, u32[]{:S(2)}) collective-permute-start(f32[6,128,128]{2,1,0:T(8,128)S(1)} %collective-permute-done.16), channel_id=1, source_target_pairs={{0,64},{16,80},{32,96},{48,112},{64,0},{80,16},{96,32},{112,48},{1... | collective-permute-start | bytes 1179656 | tf_op jit(solution)/shard_map/ppermute | solution.py:512
  138.5 20.0 %collective-permute-start.6 = (f32[8,128,128]{2,1,0:T(8,128)S(1)}, f32[8,128,128]{2,1,0:T(8,128)S(1)}, u32[]{:S(2)}, u32[]{:S(2)}) collective-permute-start(f32[8,128,128]{2,1,0:T(8,128)S(1)} %pad_maximum_fusion.1.refs_0_), channel_id=1, source_target_pairs={{0,16},{16,32},{32,48},{48,0},{64,80},{80,96},{96,112},{112,64},{1... | collective-permute-start | bytes 1572872 | tf_op jit(solution)/shard_map/ppermute | solution.py:499
  142.0 17.0 %collective-permute-start.7 = (f32[8,128,128]{2,1,0:T(8,128)S(1)}, f32[8,128,128]{2,1,0:T(8,128)S(1)}, u32[]{:S(2)}, u32[]{:S(2)}) collective-permute-start(f32[8,128,128]{2,1,0:T(8,128)S(1)} %pad_maximum_fusion.1.refs_0_), channel_id=1, source_target_pairs={{0,32},{16,48},{32,0},{48,16},{64,96},{80,112},{96,64},{112,80},{1... | collective-permute-start | bytes 1572872 | tf_op jit(solution)/shard_map/ppermute | solution.py:499
  156.4 30.0 %collective-permute-start.18 = (f32[2,6,128,128]{3,2,1,0:T(8,128)S(1)}, f32[2,6,128,128]{3,2,1,0:T(8,128)S(1)}, u32[]{:S(2)}, u32[]{:S(2)}) collective-permute-start(f32[2,6,128,128]{3,2,1,0:T(8,128)S(1)} %pad_maximum_fusion.in0), channel_id=1, source_target_pairs={{0,16},{16,32},{32,48},{48,0},{64,80},{80,96},{96,112},{112,64},{1... | collective-permute-start | bytes 2359304 | tf_op jit(solution)/shard_map/ppermute | solution.py:514
  158.5 1.9 collective-permute-start.12
  158.5 2.9 collective-permute-start.13
  159.1 3.7 collective-permute-start.14
  159.1 6.5 %collective-permute-start.15 = (f32[8,128,128]{2,1,0:T(8,128)S(1)}, f32[8,128,128]{2,1,0:T(8,128)S(1)}, u32[]{:S(2)}, u32[]{:S(2)}) collective-permute-start(f32[8,128,128]{2,1,0:T(8,128)S(1)} %collective-permute-done.11.refs_3_), channel_id=1, source_target_pairs={{0,1},{1,0},{2,3},{3,2},{4,5},{5,4},{6,7},{7,6},{8,9},{9,8},{10,11... | collective-permute-start | bytes 1572872 | tf_op jit(solution)/shard_map/ppermute | solution.py:500
  160.4 233.7 %collective-permute-start.21 = (f32[2,4,2,128,128]{4,3,2,1,0:T(8,128)}, f32[2,4,2,128,128]{4,3,2,1,0:T(8,128)S(1)}, u32[]{:S(2)}, u32[]{:S(2)}) collective-permute-start(f32[2,4,2,128,128]{4,3,2,1,0:T(8,128)} %copy-done.4), channel_id=1, source_target_pairs={{0,4},{1,5},{2,6},{3,7},{4,8},{5,9},{6,10},{7,11},{8,12},{9,13},{1... | collective-permute-start | bytes 3145736 | tf_op jit(solution)/shard_map/ppermute | solution.py:534
  161.4 232.8 %collective-permute-start.22 = (f32[2,4,2,128,128]{4,3,2,1,0:T(8,128)S(1)}, f32[2,4,2,128,128]{4,3,2,1,0:T(8,128)S(1)}, u32[]{:S(2)}, u32[]{:S(2)}) collective-permute-start(f32[2,4,2,128,128]{4,3,2,1,0:T(8,128)S(1)} %get-tuple-element.55), channel_id=1, source_target_pairs={{0,8},{1,9},{2,10},{3,11},{4,12},{5,13},{6,14},{7,15},{8,0},{9,1},... | collective-permute-start | bytes 3145736 | tf_op jit(solution)/shard_map/ppermute | solution.py:534
  162.8 233.4 %collective-permute-start.23 = (f32[2,4,2,128,128]{4,3,2,1,0:T(8,128)S(1)}, f32[2,4,2,128,128]{4,3,2,1,0:T(8,128)}, u32[]{:S(2)}, u32[]{:S(2)}) collective-permute-start(f32[2,4,2,128,128]{4,3,2,1,0:T(8,128)S(1)} %get-tuple-element.56), channel_id=1, source_target_pairs={{0,12},{1,13},{2,14},{3,15},{4,0},{5,1},{6,2},{7,3},{8,4},{9,5},{1... | collective-permute-start | bytes 3145736 | tf_op jit(solution)/shard_map/ppermute | solution.py:534
  165.7 218.4 %collective-permute-start.19 = (f32[2,6,128,128]{3,2,1,0:T(8,128)S(1)}, f32[2,6,128,128]{3,2,1,0:T(8,128)S(1)}, u32[]{:S(2)}, u32[]{:S(2)}) collective-permute-start(f32[2,6,128,128]{3,2,1,0:T(8,128)S(1)} %pad_maximum_fusion.in0), channel_id=1, source_target_pairs={{0,32},{16,48},{32,0},{48,16},{64,96},{80,112},{96,64},{112,80},{1... | collective-permute-start | bytes 2359304 | tf_op jit(solution)/shard_map/ppermute | solution.py:514
  186.4 197.7 %collective-permute-start.20 = (f32[2,6,128,128]{3,2,1,0:T(8,128)S(1)}, f32[2,6,128,128]{3,2,1,0:T(8,128)S(1)}, u32[]{:S(2)}, u32[]{:S(2)}) collective-permute-start(f32[2,6,128,128]{3,2,1,0:T(8,128)S(1)} %pad_maximum_fusion.in0), channel_id=1, source_target_pairs={{0,48},{16,0},{32,16},{48,32},{64,112},{80,64},{96,80},{112,96},{1... | collective-permute-start | bytes 2359304 | tf_op jit(solution)/shard_map/ppermute | solution.py:514
  384.0 7.8 %copy-start.7 = (f32[128,128]{1,0:T(8,128)}, f32[128,128]{1,0:T(8,128)S(1)}, u32[]{:S(2)}) copy-start(f32[128,128]{1,0:T(8,128)S(1)} %get-tuple-element.52.own_ref) | copy-start | bytes 196612
  393.0 1.2 copy-start.6
  (5 other events, 5.1 us)
Sparse Core Ops, SparseCore 0:
  113.8 53.5 all-gather.2

commit v2 on v1

--- a/solution.py
+++ b/solution.py
@@ -408,19 +408,21 @@
                     diag_ref[pl.ds(16 * s + q, 1), :]
                 )
 
-        def add(k, in_ref, t):
-            c, h, n = k // 8, (k // 2) % 4, k % 2
-            l = local_row(map_ref, c, h, n, p)
-            s = local_col(map_ref, c, t, q)
-
-            @pl.when(l // group == step)
-            def _():
-                rows = pl.ds(pl.multiple_of((l % group) * BLOCK, BLOCK), BLOCK)
-                cols = pl.ds(pl.multiple_of(s * BLOCK, BLOCK), BLOCK)
-                out_ref[rows, cols] += in_ref[c, h, n]
-
-        for d, in_ref in enumerate((in0, in1, in2, in3)):
-            pl.loop(0, 16)(functools.partial(add, in_ref=in_ref, t=(q // 4 + 4 - d) % 4))
+        in_refs = (in0, in1, in2, in3)
+        for c in range(2):
+            places = [local_col(map_ref, c, (q // 4 + 4 - d) % 4, q) for d in range(4)]
+
+            def add(k):
+                l = local_row(map_ref, c, k // 2, k % 2, p)
+
+                @pl.when(l // group == step)
+                def _():
+                    rows = pl.ds(pl.multiple_of((l % group) * BLOCK, BLOCK), BLOCK)
+                    for d in range(4):
+                        cols = pl.ds(pl.multiple_of(places[d] * BLOCK, BLOCK), BLOCK)
+                        out_ref[rows, cols] += in_refs[d][c, k // 2, k % 2]
+
+            pl.loop(0, 8)(add)
 
         @pl.when(q < HEAD)
         def _():
@@ -524,9 +526,9 @@
     summed, along_z, twins = gather_head(head_terms)
     summed, *terms = lax.optimization_barrier([summed, *terms])
     behind = [lax.ppermute(terms[d], "pcol", ahead_x(d)) for d in (1, 2, 3)]
-    *behind, last = lax.optimization_barrier([*behind, along_z[3]])
+    behind, along_z = lax.optimization_barrier((behind, along_z))
     piece = terms[0] + behind[0] + behind[1] + behind[2]
-    gathered = along_z[:3] + [last] + twins
+    gathered = along_z + twins
     blocks = pack_cols(sent, child_map)
     piece, *ahead = lax.optimization_barrier([piece, *blocks[1:]])
     arrived = [blocks[0]]

time: 428 us -> 419 us (0.979)
  the two profiles are of different devices: /device:TPU:40 before, /device:TPU:0 now
where the time goes in v2:
time: 419 us; the launch traced here: 417 us
  Pallas kernels  213 us (51%)
  waiting for transfers between devices  60.9 us (15%)
  starting transfers between devices  60.5 us (14%)
  blocking collectives  59.4 us (14%)
  between operations  13.6 us (3%)
  local copies, waits for them, and re-layouts  8.28 us (2%)
    pallas_call x1, Pallas kernels, head_factor(): pl.pallas_call(kernel, out_shape=[jax.ShapeDtypeStruct((size, size), BF16...  183 us
    all_to_all x1, blocking collectives, per_device(): lax.all_to_all(sent, BOTH, 0, 0, axis_index_groups=PLANE_GROUPS, tiled=True)  59.4 us
    ppermute x1, starting transfers between devices, gather_columns(): other = lax.ppermute(turned, 'prow', [(p, p ^ 4) for p in range(8)])  23 us
    ppermute x3, waiting for transfers between devices, gather_columns(): return [held] + [lax.ppermute(held, 'prow', ahead_z(d)) for d in (1, 2, 3)]  21.3 us
    ppermute x1, waiting for transfers between devices, gather_columns(): other = lax.ppermute(turned, 'prow', [(p, p ^ 4) for p in range(8)])  17.9 us
    pallas_call x1, Pallas kernels, finish(): pl.pallas_call(kernel, out_shape=jax.ShapeDtypeStruct((12 * BLOCK, wide),...  16.7 us
    ppermute x3, waiting for transfers between devices, per_device(): behind = [lax.ppermute(terms[d], 'pcol', ahead_x(d)) for d in (1, 2, 3)]  11.2 us
  transfers between devices with their start and end apart: 25, of which 14 were waited for; matrix products, arithmetic and copies ran while one was open for 0% of the time, Pallas kernels for 46%

profile of v2, /device:TPU:0, one launch (start us, length us, event | category | flops | bytes accessed | tf_op | source)
XLA Modules:
  0.0 416.8 jit_solution(10203932057165053991)
XLA Ops:
  7.3 2.2 copy-done
  9.5 2.5 pack_rows.1
  12.0 59.4 %all_to_all.5 = f32[64,128,128]{2,1,0:T(8,128)S(1)} all-to-all(f32[64,128,128]{2,1,0:T(8,128)S(1)} %bitcast.8), channel_id=1, replica_groups={{0,16,32,48,64,80,96,112,1,17,33,49,65,81,97,113,2,18,34,50,66,82,98,11..., dimensions={0} | all-to-all | bytes 8388608 | tf_op jit(solution)/shard_map/all_to_all | solution.py:523
  71.5 1.4 panel_terms.1
  72.9 1.3 collective-permute-start
  74.1 2.7 collective-permute-start.1
  76.8 2.0 collective-permute-start.2
  78.9 1.7 collective-permute-done
  80.5 1.4 collective-permute-done.1
  82.0 1.5 collective-permute-start.3
  84.3 2.3 collective-permute-start.7
  86.7 1.4 collective-permute-start.8
  88.1 2.1 collective-permute-done.6
  90.2 1.4 collective-permute-done.7
  92.0 2.6 collective-permute-start.10
  94.6 2.0 collective-permute-start.11
  96.7 3.4 collective-permute-start.4
  100.1 1.6 collective-permute-start.5
  101.7 1.4 pack_cols.1
  104.1 2.8 collective-permute-done.4
  106.9 8.4 %collective-permute-done.5 = f32[6,128,128]{2,1,0:T(8,128)S(1)} collective-permute-done((f32[6,128,128]{2,1,0:T(8,128)S(1)}, f32[6,128,128]{2,1,0:T(8,128)S(1)}, u32[]{:S(2)}, u32[]{:S(2)}) %collective-permute-start.5) | collective-permute-done | bytes 393248 | tf_op jit(solution)/shard_map/ppermute | solution.py:528
  117.3 1.7 collective-permute-start.16
  119.0 23.0 %collective-permute-start.17 = (f32[6,128,128]{2,1,0:T(8,128)S(1)}, f32[6,128,128]{2,1,0:T(8,128)S(1)}, u32[]{:S(2)}, u32[]{:S(2)}) collective-permute-start(f32[6,128,128]{2,1,0:T(8,128)S(1)} %collective-permute-done.16), channel_id=1, source_target_pairs={{0,64},{16,80},{32,96},{48,112},{64,0},{80,16},{96,32},{112,48},{1... | collective-permute-start | bytes 1179656 | tf_op jit(solution)/shard_map/ppermute | solution.py:514
  142.0 17.9 %collective-permute-done.17 = f32[6,128,128]{2,1,0:T(8,128)S(1)} collective-permute-done((f32[6,128,128]{2,1,0:T(8,128)S(1)}, f32[6,128,128]{2,1,0:T(8,128)S(1)}, u32[]{:S(2)}, u32[]{:S(2)}) %collective-permute-start.17) | collective-permute-done | bytes 393248 | tf_op jit(solution)/shard_map/ppermute | solution.py:514
  160.0 1.6 collective-permute-start.18
  162.6 1.6 collective-permute-done.12.refs_4_
  165.0 5.6 %collective-permute-start.22 = (f32[2,4,2,128,128]{4,3,2,1,0:T(8,128)S(1)}, f32[2,4,2,128,128]{4,3,2,1,0:T(8,128)S(1)}, u32[]{:S(2)}, u32[]{:S(2)}) collective-permute-start(f32[2,4,2,128,128]{4,3,2,1,0:T(8,128)S(1)} %get-tuple-element.61), channel_id=1, source_target_pairs={{0,8},{1,9},{2,10},{3,11},{4,12},{5,13},{6,14},{7,15},{8,0},{9,1},... | collective-permute-start | bytes 3145736 | tf_op jit(solution)/shard_map/ppermute | solution.py:536
  170.9 5.5 %collective-permute-start.19 = (f32[2,6,128,128]{3,2,1,0:T(8,128)S(1)}, f32[2,6,128,128]{3,2,1,0:T(8,128)S(1)}, u32[]{:S(2)}, u32[]{:S(2)}) collective-permute-start(f32[2,6,128,128]{3,2,1,0:T(8,128)S(1)} %pad_maximum_fusion.in0), channel_id=1, source_target_pairs={{0,32},{16,48},{32,0},{48,16},{64,96},{80,112},{96,64},{112,80},{1... | collective-permute-start | bytes 2359304 | tf_op jit(solution)/shard_map/ppermute | solution.py:516
  176.4 21.3 %collective-permute-done.18.in1 = f32[2,6,128,128]{3,2,1,0:T(8,128)S(1)} collective-permute-done((f32[2,6,128,128]{3,2,1,0:T(8,128)S(1)}, f32[2,6,128,128]{3,2,1,0:T(8,128)S(1)}, u32[]{:S(2)}, u32[]{:S(2)}) %collective-permute-start.18) | collective-permute-done | bytes 786464 | tf_op jit(solution)/shard_map/ppermute | solution.py:516
  197.7 183.4 %head_factor.1 = (bf16[1024,1024]{1,0:T(8,128)(2,1)S(1)}, bf16[1024,1024]{1,0:T(8,128)(2,1)S(1)}, f32[128,128]{1,0:T(8,128)S(1)}) custom-call(f32[8,128,128]{2,1,0:T(8,128)S(1)} %pad_maximum_fusion.1.refs_0_, f32[8,128,128]{2,1,0:T(8,128)} %collective-permute-done.9.refs_1_, f32[8,128,128]{2,1,0:T(8,128)S(1)} %collective-permute-done.10.refs_2_, ...), custom_call_target="tpu_custom_call" | custom-call | flops 20000000000 | bytes 8388608 | tf_op jit(solution)/shard_map/head_factor/pallas_call | solution.py:330
  381.2 7.7 %solve_columns.1 = (bf16[768,1024]{1,0:T(8,128)(2,1)S(1)}, bf16[768,1024]{1,0:T(8,128)(2,1)S(1)}) custom-call(bf16[1024,1024]{1,0:T(8,128)(2,1)S(1)} %get-tuple-element.46.wh, bf16[1024,1024]{1,0:T(8,128)(2,1)S(1)} %get-tuple-element.47.wl, f32[2,6,128,128]{3,2,1,0:T(8,128)S(1)} %pad_maximum_fusion.in0, f32[2,6,128,128]{3,2,1,0:T(8,128)S(1)} %collective-permute-done.18.in1, ...), custom_call_target="tpu_custom_call" | custom-call | flops 8000000000 | bytes 10485760 | tf_op jit(solution)/shard_map/solve_columns/pallas_call | solution.py:378
  393.3 16.7 %finish.1 = f32[1536,768]{1,0:T(8,128)} custom-call(s32[128]{0:T(128)} %copy-done.2, bf16[768,1024]{1,0:T(8,128)(2,1)} %copy-done.5, bf16[768,1024]{1,0:T(8,128)(2,1)} %copy-done.6, f32[128,128]{1,0:T(8,128)} %copy-done.7, f32[96,128]{1,0:T(8,128)} %bitcast.11, f32[2,4,2,128,128]{4,3,2,1,0:T(8,128)} %copy-done.3, f32[2,4,2,128,128]{4,3,2,1,0:T(8,128)} %copy-done.8, ...), custom_call_target="tpu_custom_call" | custom-call | flops 8000000000 | bytes 25165824 | tf_op jit(solution)/shard_map/finish/pallas_call | solution.py:449
  (56 shorter events, 11.6 us)
Async XLA Ops:
  6.5 386.8 %all-gather.3.cloned.1.call-start = ((), (), s32[]{:S(2)}) async-start(), calls=%async_computation.1 | async-start | bytes 6684672 | tf_op jit(solution)/shard_map/all_gather | solution.py:537
  7.3 2.2 copy-start
  9.5 92.2 %copy-start.2 = (s32[128]{0:T(128)}, s32[128]{0:T(128)S(1)}, u32[]{:S(2)}) copy-start(s32[128]{0:T(128)S(1)} %reshape.12.map_ref) | copy-start | bytes 1540
  9.5 62.0 %slice-start = ((s8[4718592]{0:T(1024)(128)(4,1)}), s8[4194304]{0:T(1024)(128)(4,1)S(1)}, s32[]{:S(2)}) async-start(s8[4718592]{0:T(1024)(128)(4,1)} %bitcast.9), calls=%async_computation.2 | async-start | bytes 8388608
  12.0 59.5 %slice-start.1 = ((s8[4718592]{0:T(1024)(128)(4,1)}), s8[524288]{0:T(1024)(128)(4,1)S(1)}, s32[]{:S(2)}) async-start(s8[4718592]{0:T(1024)(128)(4,1)} %bitcast.9), calls=%async_computation.3 | async-start | bytes 1048576
  12.0 59.5 %copy-start.1 = (f32[12288]{0:T(1024)S(1)}, f32[12288]{0:T(1024)}, u32[]{:S(2)}) copy-start(f32[12288]{0:T(1024)} %param.5) | copy-start | bytes 147460
  72.9 7.7 %collective-permute-start = (f32[2,128,128]{2,1,0:T(8,128)S(1)}, f32[2,128,128]{2,1,0:T(8,128)S(1)}, u32[]{:S(2)}, u32[]{:S(2)}) collective-permute-start(f32[2,128,128]{2,1,0:T(8,128)S(1)} %get-tuple-element.34), channel_id=1, source_target_pairs={{0,4},{1,5},{2,6},{3,7},{4,8},{5,9},{6,10},{7,11},{8,12},{9,13},{1... | collective-permute-start | bytes 393224 | tf_op jit(solution)/shard_map/ppermute | solution.py:497
  74.1 7.8 %collective-permute-start.1 = (f32[2,128,128]{2,1,0:T(8,128)S(1)}, f32[2,128,128]{2,1,0:T(8,128)S(1)}, u32[]{:S(2)}, u32[]{:S(2)}) collective-permute-start(f32[2,128,128]{2,1,0:T(8,128)S(1)} %get-tuple-element.34), channel_id=1, source_target_pairs={{0,8},{1,9},{2,10},{3,11},{4,12},{5,13},{6,14},{7,15},{8,0},{9,1},... | collective-permute-start | bytes 393224 | tf_op jit(solution)/shard_map/ppermute | solution.py:497
  76.8 5.2 %collective-permute-start.2 = (f32[2,128,128]{2,1,0:T(8,128)S(1)}, f32[2,128,128]{2,1,0:T(8,128)S(1)}, u32[]{:S(2)}, u32[]{:S(2)}) collective-permute-start(f32[2,128,128]{2,1,0:T(8,128)S(1)} %get-tuple-element.34), channel_id=1, source_target_pairs={{0,12},{1,13},{2,14},{3,15},{4,0},{5,1},{6,2},{7,3},{8,4},{9,5},{1... | collective-permute-start | bytes 393224 | tf_op jit(solution)/shard_map/ppermute | solution.py:497
  82.0 18.1 %collective-permute-start.3 = (f32[6,128,128]{2,1,0:T(8,128)S(1)}, f32[6,128,128]{2,1,0:T(8,128)S(1)}, u32[]{:S(2)}, u32[]{:S(2)}) collective-permute-start(f32[6,128,128]{2,1,0:T(8,128)S(1)} %get-tuple-element.39), channel_id=1, source_target_pairs={{0,4},{1,5},{2,6},{3,7},{4,8},{5,9},{6,10},{7,11},{8,12},{9,13},{1... | collective-permute-start | bytes 1179656 | tf_op jit(solution)/shard_map/ppermute | solution.py:528
  83.5 6.7 %collective-permute-start.6 = (f32[2,128,128]{2,1,0:T(8,128)S(1)}, f32[2,128,128]{2,1,0:T(8,128)S(1)}, u32[]{:S(2)}, u32[]{:S(2)}) collective-permute-start(f32[2,128,128]{2,1,0:T(8,128)S(1)} %add_add_fusion.1), channel_id=1, source_target_pairs={{0,2},{1,3},{4,6},{5,7},{8,10},{9,11},{12,14},{13,15},{16,18},{17,... | collective-permute-start | bytes 393224 | tf_op jit(solution)/shard_map/ppermute | solution.py:499
  84.3 7.3 %collective-permute-start.7 = (f32[2,128,128]{2,1,0:T(8,128)S(1)}, f32[2,128,128]{2,1,0:T(8,128)S(1)}, u32[]{:S(2)}, u32[]{:S(2)}) collective-permute-start(f32[2,128,128]{2,1,0:T(8,128)S(1)} %add_add_fusion.1), channel_id=1, source_target_pairs={{0,64},{1,65},{4,68},{5,69},{8,72},{9,73},{12,76},{13,77},{16,80},... | collective-permute-start | bytes 393224 | tf_op jit(solution)/shard_map/ppermute | solution.py:499
  86.7 5.3 %collective-permute-start.8 = (f32[2,128,128]{2,1,0:T(8,128)S(1)}, f32[2,128,128]{2,1,0:T(8,128)S(1)}, u32[]{:S(2)}, u32[]{:S(2)}) collective-permute-start(f32[2,128,128]{2,1,0:T(8,128)S(1)} %add_add_fusion.1), channel_id=1, source_target_pairs={{0,66},{1,67},{4,70},{5,71},{8,74},{9,75},{12,78},{13,79},{16,82},... | collective-permute-start | bytes 393224 | tf_op jit(solution)/shard_map/ppermute | solution.py:499
  92.0 23.3 %collective-permute-start.10 = (f32[8,128,128]{2,1,0:T(8,128)S(1)}, f32[8,128,128]{2,1,0:T(8,128)S(1)}, u32[]{:S(2)}, u32[]{:S(2)}) collective-permute-start(f32[8,128,128]{2,1,0:T(8,128)S(1)} %pad_maximum_fusion.1.refs_0_), channel_id=1, source_target_pairs={{0,32},{16,48},{32,0},{48,16},{64,96},{80,112},{96,64},{112,80},{1... | collective-permute-start | bytes 1572872 | tf_op jit(solution)/shard_map/ppermute | solution.py:501
  94.6 21.7 %collective-permute-start.11 = (f32[8,128,128]{2,1,0:T(8,128)S(1)}, f32[8,128,128]{2,1,0:T(8,128)}, u32[]{:S(2)}, u32[]{:S(2)}) collective-permute-start(f32[8,128,128]{2,1,0:T(8,128)S(1)} %pad_maximum_fusion.1.refs_0_), channel_id=1, source_target_pairs={{0,48},{16,0},{32,16},{48,32},{64,112},{80,64},{96,80},{112,96},{1... | collective-permute-start | bytes 1572872 | tf_op jit(solution)/shard_map/ppermute | solution.py:501
  96.6 19.9 %collective-permute-start.9 = (f32[8,128,128]{2,1,0:T(8,128)S(1)}, f32[8,128,128]{2,1,0:T(8,128)}, u32[]{:S(2)}, u32[]{:S(2)}) collective-permute-start(f32[8,128,128]{2,1,0:T(8,128)S(1)} %pad_maximum_fusion.1.refs_0_), channel_id=1, source_target_pairs={{0,16},{16,32},{32,48},{48,0},{64,80},{80,96},{96,112},{112,64},{1... | collective-permute-start | bytes 1572872 | tf_op jit(solution)/shard_map/ppermute | solution.py:501
  96.7 10.3 %collective-permute-start.4 = (f32[6,128,128]{2,1,0:T(8,128)S(1)}, f32[6,128,128]{2,1,0:T(8,128)S(1)}, u32[]{:S(2)}, u32[]{:S(2)}) collective-permute-start(f32[6,128,128]{2,1,0:T(8,128)S(1)} %get-tuple-element.40), channel_id=1, source_target_pairs={{0,8},{1,9},{2,10},{3,11},{4,12},{5,13},{6,14},{7,15},{8,0},{9,1},... | collective-permute-start | bytes 1179656 | tf_op jit(solution)/shard_map/ppermute | solution.py:528
  100.1 15.2 %collective-permute-start.5 = (f32[6,128,128]{2,1,0:T(8,128)S(1)}, f32[6,128,128]{2,1,0:T(8,128)S(1)}, u32[]{:S(2)}, u32[]{:S(2)}) collective-permute-start(f32[6,128,128]{2,1,0:T(8,128)S(1)} %get-tuple-element.41), channel_id=1, source_target_pairs={{0,12},{1,13},{2,14},{3,15},{4,0},{5,1},{6,2},{7,3},{8,4},{9,5},{1... | collective-permute-start | bytes 1179656 | tf_op jit(solution)/shard_map/ppermute | solution.py:528
  104.1 12.3 %copy-start.4 = (f32[2,4,2,128,128]{4,3,2,1,0:T(8,128)}, f32[2,4,2,128,128]{4,3,2,1,0:T(8,128)S(1)}, u32[]{:S(2)}) copy-start(f32[2,4,2,128,128]{4,3,2,1,0:T(8,128)S(1)} %get-tuple-element.60) | copy-start | bytes 3145732
  117.3 1.7 collective-permute-start.16
  119.0 40.9 %collective-permute-start.17 = (f32[6,128,128]{2,1,0:T(8,128)S(1)}, f32[6,128,128]{2,1,0:T(8,128)S(1)}, u32[]{:S(2)}, u32[]{:S(2)}) collective-permute-start(f32[6,128,128]{2,1,0:T(8,128)S(1)} %collective-permute-done.16), channel_id=1, source_target_pairs={{0,64},{16,80},{32,96},{48,112},{64,0},{80,16},{96,32},{112,48},{1... | collective-permute-start | bytes 1179656 | tf_op jit(solution)/shard_map/ppermute | solution.py:514
  160.0 37.8 %collective-permute-start.18 = (f32[2,6,128,128]{3,2,1,0:T(8,128)S(1)}, f32[2,6,128,128]{3,2,1,0:T(8,128)S(1)}, u32[]{:S(2)}, u32[]{:S(2)}) collective-permute-start(f32[2,6,128,128]{3,2,1,0:T(8,128)S(1)} %pad_maximum_fusion.in0), channel_id=1, source_target_pairs={{0,16},{16,32},{32,48},{48,0},{64,80},{80,96},{96,112},{112,64},{1... | collective-permute-start | bytes 2359304 | tf_op jit(solution)/shard_map/ppermute | solution.py:516
  161.6 2.6 collective-permute-start.12
  161.6 3.4 collective-permute-start.13
  162.1 8.5 %collective-permute-start.14 = (f32[8,128,128]{2,1,0:T(8,128)S(1)}, f32[8,128,128]{2,1,0:T(8,128)S(1)}, u32[]{:S(2)}, u32[]{:S(2)}) collective-permute-start(f32[8,128,128]{2,1,0:T(8,128)S(1)} %collective-permute-done.10.refs_2_), channel_id=1, source_target_pairs={{0,1},{1,0},{2,3},{3,2},{4,5},{5,4},{6,7},{7,6},{8,9},{9,8},{10,11... | collective-permute-start | bytes 1572872 | tf_op jit(solution)/shard_map/ppermute | solution.py:502
  162.1 8.8 %collective-permute-start.15 = (f32[8,128,128]{2,1,0:T(8,128)}, f32[8,128,128]{2,1,0:T(8,128)S(1)}, u32[]{:S(2)}, u32[]{:S(2)}) collective-permute-start(f32[8,128,128]{2,1,0:T(8,128)} %collective-permute-done.11.refs_3_), channel_id=1, source_target_pairs={{0,1},{1,0},{2,3},{3,2},{4,5},{5,4},{6,7},{7,6},{8,9},{9,8},{10,11... | collective-permute-start | bytes 1572872 | tf_op jit(solution)/shard_map/ppermute | solution.py:502
  164.2 227.1 %collective-permute-start.21 = (f32[2,4,2,128,128]{4,3,2,1,0:T(8,128)}, f32[2,4,2,128,128]{4,3,2,1,0:T(8,128)S(1)}, u32[]{:S(2)}, u32[]{:S(2)}) collective-permute-start(f32[2,4,2,128,128]{4,3,2,1,0:T(8,128)} %copy-done.4), channel_id=1, source_target_pairs={{0,4},{1,5},{2,6},{3,7},{4,8},{5,9},{6,10},{7,11},{8,12},{9,13},{1... | collective-permute-start | bytes 3145736 | tf_op jit(solution)/shard_map/ppermute | solution.py:536
  165.0 226.3 %collective-permute-start.22 = (f32[2,4,2,128,128]{4,3,2,1,0:T(8,128)S(1)}, f32[2,4,2,128,128]{4,3,2,1,0:T(8,128)S(1)}, u32[]{:S(2)}, u32[]{:S(2)}) collective-permute-start(f32[2,4,2,128,128]{4,3,2,1,0:T(8,128)S(1)} %get-tuple-element.61), channel_id=1, source_target_pairs={{0,8},{1,9},{2,10},{3,11},{4,12},{5,13},{6,14},{7,15},{8,0},{9,1},... | collective-permute-start | bytes 3145736 | tf_op jit(solution)/shard_map/ppermute | solution.py:536
  170.6 222.7 %collective-permute-start.23 = (f32[2,4,2,128,128]{4,3,2,1,0:T(8,128)S(1)}, f32[2,4,2,128,128]{4,3,2,1,0:T(8,128)}, u32[]{:S(2)}, u32[]{:S(2)}) collective-permute-start(f32[2,4,2,128,128]{4,3,2,1,0:T(8,128)S(1)} %get-tuple-element.62), channel_id=1, source_target_pairs={{0,12},{1,13},{2,14},{3,15},{4,0},{5,1},{6,2},{7,3},{8,4},{9,5},{1... | collective-permute-start | bytes 3145736 | tf_op jit(solution)/shard_map/ppermute | solution.py:536
  170.9 210.3 %collective-permute-start.19 = (f32[2,6,128,128]{3,2,1,0:T(8,128)S(1)}, f32[2,6,128,128]{3,2,1,0:T(8,128)S(1)}, u32[]{:S(2)}, u32[]{:S(2)}) collective-permute-start(f32[2,6,128,128]{3,2,1,0:T(8,128)S(1)} %pad_maximum_fusion.in0), channel_id=1, source_target_pairs={{0,32},{16,48},{32,0},{48,16},{64,96},{80,112},{96,64},{112,80},{1... | collective-permute-start | bytes 2359304 | tf_op jit(solution)/shard_map/ppermute | solution.py:516
  197.7 183.5 %collective-permute-start.20 = (f32[2,6,128,128]{3,2,1,0:T(8,128)S(1)}, f32[2,6,128,128]{3,2,1,0:T(8,128)S(1)}, u32[]{:S(2)}, u32[]{:S(2)}) collective-permute-start(f32[2,6,128,128]{3,2,1,0:T(8,128)S(1)} %pad_maximum_fusion.in0), channel_id=1, source_target_pairs={{0,48},{16,0},{32,16},{48,32},{64,112},{80,64},{96,80},{112,96},{1... | collective-permute-start | bytes 2359304 | tf_op jit(solution)/shard_map/ppermute | solution.py:516
  381.1 7.8 %copy-start.7 = (f32[128,128]{1,0:T(8,128)}, f32[128,128]{1,0:T(8,128)S(1)}, u32[]{:S(2)}) copy-start(f32[128,128]{1,0:T(8,128)S(1)} %get-tuple-element.58.own_ref) | copy-start | bytes 196612
  (5 other events, 5.3 us)
Sparse Core Ops, SparseCore 0:
  117.4 59.4 all-gather.2

commit v3 on v2

--- a/solution.py
+++ b/solution.py
@@ -18,43 +18,43 @@
 
 
 def pack_rows(child, child_map):
-    def kernel(map_ref, child_ref, out_ref, buf, turned, sems):
+    def kernel(map_ref, child_ref, even_ref, odd_ref, buf, turned, sems):
         c = lax.axis_index("prow") // 4
         shift = map_ref[c * 64] % 16
 
-        def fetch(i):
+        def fetch(k):
+            i = (k - shift + 16) % 16
             rows = pl.ds(pl.multiple_of(i * BLOCK, BLOCK), BLOCK)
-            return pltpu.make_async_copy(child_ref.at[rows], buf.at[i], sems.at[0, i])
-
-        def store(i):
-            residue = (i + shift) % 16
-            return pltpu.make_async_copy(
-                turned.at[i], out_ref.at[:, residue % 8, residue // 8], sems.at[1, i]
-            )
-
-        def forward(i):
-            fetch(i).wait()
+            return pltpu.make_async_copy(child_ref.at[rows], buf.at[k], sems.at[0, k])
+
+        def store(k, out_ref):
+            return pltpu.make_async_copy(turned.at[k], out_ref.at[:, k % 8], sems.at[1, k])
+
+        def forward(k, out_ref):
+            fetch(k).wait()
             for w in range(4):
                 b = (w - shift + 16) % 4
-                turned[i, w] = buf[i, :, pl.ds(pl.multiple_of(b * BLOCK, BLOCK), BLOCK)]
-            store(i).start()
-
-        pl.loop(0, 16)(lambda i: fetch(i).start())
-        pl.loop(0, 16)(forward)
-        pl.loop(0, 16)(lambda i: store(i).wait())
+                turned[k, w] = buf[k, :, pl.ds(pl.multiple_of(b * BLOCK, BLOCK), BLOCK)]
+            store(k, out_ref).start()
+
+        pl.loop(0, 16)(lambda k: fetch(k).start())
+        pl.loop(0, 8)(lambda k: forward(k, even_ref))
+        pl.loop(8, 16)(lambda k: forward(k, odd_ref))
+        pl.loop(0, 8)(lambda k: store(k, even_ref).wait())
+        pl.loop(8, 16)(lambda k: store(k, odd_ref).wait())
 
     return pl.pallas_call(
         kernel,
-        out_shape=jax.ShapeDtypeStruct((4, 8, 2, BLOCK, BLOCK), F32),
+        out_shape=[jax.ShapeDtypeStruct((4, 8, BLOCK, BLOCK), F32)] * 2,
         in_specs=[pl.BlockSpec(memory_space=pltpu.SMEM), pl.BlockSpec(memory_space=pl.ANY)],
-        out_specs=pl.BlockSpec(memory_space=pl.ANY),
+        out_specs=[pl.BlockSpec(memory_space=pl.ANY)] * 2,
         scratch_shapes=[
             pltpu.VMEM((16, BLOCK, 4 * BLOCK), F32),
             pltpu.VMEM((16, 4, BLOCK, BLOCK), F32),
             pltpu.SemaphoreType.DMA((2, 16)),
         ],
         compiler_params=pltpu.CompilerParams(vmem_limit_bytes=16 * MIB),
-        cost_estimate=pl.CostEstimate(flops=0, bytes_accessed=8 * MIB, transcendentals=0),
+        cost_estimate=pl.CostEstimate(flops=1, bytes_accessed=1, transcendentals=0),
         name="pack_rows",
     )(child_map, child)
 
@@ -84,14 +84,14 @@
 
     return pl.pallas_call(
         kernel,
-        out_shape=[jax.ShapeDtypeStruct((2, 4, 2, BLOCK, BLOCK), F32)] * 4,
+        out_shape=[jax.ShapeDtypeStruct((2, 4, BLOCK, BLOCK), F32)] * 4,
         in_specs=[pl.BlockSpec(memory_space=pltpu.SMEM), pl.BlockSpec(memory_space=pl.ANY)],
         out_specs=[pl.BlockSpec(memory_space=pl.ANY)] * 4,
         scratch_shapes=[
-            pltpu.VMEM((8, 4, 2, BLOCK, BLOCK), F32), pltpu.SemaphoreType.DMA((2, 8))
+            pltpu.VMEM((8, 4, BLOCK, BLOCK), F32), pltpu.SemaphoreType.DMA((2, 8))
         ],
         compiler_params=pltpu.CompilerParams(vmem_limit_bytes=16 * MIB),
-        cost_estimate=pl.CostEstimate(flops=0, bytes_accessed=8 * MIB, transcendentals=0),
+        cost_estimate=pl.CostEstimate(flops=1, bytes_accessed=1, transcendentals=0),
         name="pack_cols",
     )(child_map, arrived)
 
@@ -113,7 +113,7 @@
     return map_ref[c * 64 + 16 * t + (q - shift + 16) % 16] // 16
 
 
-def panel_terms(front, diagonal, arrived, child_map):
+def panel_terms(front, diagonal, arrived, child_map, n):
     def kernel(map_ref, front_ref, diag_ref, in_ref, *refs):
         out_refs, head_ref, (total, buf, sems) = refs[:4], refs[4], refs[5:]
         p, q = lax.axis_index("prow"), lax.axis_index("pcol")
@@ -133,12 +133,15 @@
 
         @pl.when(x < 2)
         def _():
-            for l in range(12):
-                total[l % 2 * 2 + x, l // 2] = front_ref[l * BLOCK : (l + 1) * BLOCK, :]
-
-        @pl.when(p == q)
-        def _():
-            total[x, 0] += diag_block(diag_ref[pl.ds(q, 1), :])
+            for l in range(6):
+                at = (2 * l + n) * BLOCK
+                total[x, l] = front_ref[at : at + BLOCK, :]
+
+        if n == 0:
+
+            @pl.when(p == q)
+            def _():
+                total[x, 0] += diag_block(diag_ref[pl.ds(q, 1), :])
 
         for k in range(4):
             e, c = k // 2, k % 2
@@ -146,14 +149,13 @@
 
             @pl.when(chosen[k])
             def _():
-                def add(i):
-                    l = local_row(map_ref, c, i // 2, i % 2, p)
-                    total[l % 2 * 2 + e, l // 2] += buf[k, i // 2, i % 2]
-
-                pl.loop(0, 8)(add)
+                def add(h):
+                    total[e, local_row(map_ref, c, h, n, p) // 2] += buf[k, h]
+
+                pl.loop(0, 4)(add)
 
         for d in range(4):
-            out_refs[d][...] = total[(x + d) % 4]
+            out_refs[d][...] = total[(x + d) % 2]
         for e in range(2):
             head_ref[e] = total[e, 0]
 
@@ -171,12 +173,12 @@
         out_specs=[pl.BlockSpec((6, BLOCK, BLOCK), lambda i: (0, 0, 0))] * 4
         + [pl.BlockSpec((2, BLOCK, BLOCK), lambda i: (0, 0, 0))],
         scratch_shapes=[
-            pltpu.VMEM((4, 6, BLOCK, BLOCK), F32),
-            pltpu.VMEM((4, 4, 2, BLOCK, BLOCK), F32),
+            pltpu.VMEM((2, 6, BLOCK, BLOCK), F32),
+            pltpu.VMEM((4, 4, BLOCK, BLOCK), F32),
             pltpu.SemaphoreType.DMA((4,)),
         ],
         compiler_params=pltpu.CompilerParams(vmem_limit_bytes=24 * MIB),
-        cost_estimate=pl.CostEstimate(flops=0, bytes_accessed=5 * MIB, transcendentals=0),
+        cost_estimate=pl.CostEstimate(flops=1, bytes_accessed=1, transcendentals=0),
         name="panel_terms",
     )(child_map, front, diagonal, arrived)
 
@@ -340,9 +342,7 @@
         + [pltpu.VMEM((wide, wide), F32)] * 2
         + [pltpu.VMEM((wide, 2 * wide), F32)],
         compiler_params=pltpu.CompilerParams(vmem_limit_bytes=40 * MIB),
-        cost_estimate=pl.CostEstimate(
-            flops=20_000_000_000, bytes_accessed=8 * MIB, transcendentals=0
-        ),
+        cost_estimate=pl.CostEstimate(flops=1, bytes_accessed=1, transcendentals=0),
         name="head_factor",
     )(*gathered)
 
@@ -382,9 +382,7 @@
         out_specs=[vmem] * 2,
         scratch_shapes=[pltpu.VMEM((wide, size), BF16)] * 4,
         compiler_params=pltpu.CompilerParams(vmem_limit_bytes=32 * MIB),
-        cost_estimate=pl.CostEstimate(
-            flops=8_000_000_000, bytes_accessed=10 * MIB, transcendentals=0
-        ),
+        cost_estimate=pl.CostEstimate(flops=1, bytes_accessed=1, transcendentals=0),
         name="solve_columns",
     )(*inverse, *col_panel)
 
@@ -393,8 +391,9 @@
     size, group, wide = HEAD * BLOCK, 4, 6 * BLOCK
 
     def kernel(
-        map_ref, sh, sl, own_ref, diag_ref, in0, in1, in2, in3, row_ref, front_ref, out_ref
+        map_ref, sh, sl, own_ref, diag_ref, *refs
     ):
+        in_refs, (row_ref, front_ref, out_ref) = refs[:8], refs[8:]
         step = pl.program_id(0)
         p, q = lax.axis_index("prow"), lax.axis_index("pcol")
         out_ref[...] = front_ref[...]
@@ -408,21 +407,21 @@
                     diag_ref[pl.ds(16 * s + q, 1), :]
                 )
 
-        in_refs = (in0, in1, in2, in3)
         for c in range(2):
             places = [local_col(map_ref, c, (q // 4 + 4 - d) % 4, q) for d in range(4)]
 
-            def add(k):
-                l = local_row(map_ref, c, k // 2, k % 2, p)
+            def add(k, n):
+                l = local_row(map_ref, c, k, n, p)
 
                 @pl.when(l // group == step)
                 def _():
                     rows = pl.ds(pl.multiple_of((l % group) * BLOCK, BLOCK), BLOCK)
                     for d in range(4):
                         cols = pl.ds(pl.multiple_of(places[d] * BLOCK, BLOCK), BLOCK)
-                        out_ref[rows, cols] += in_refs[d][c, k // 2, k % 2]
-
-            pl.loop(0, 8)(add)
+                        out_ref[rows, cols] += in_refs[4 * n + d][c, k]
+
+            for n in range(2):
+                pl.loop(0, 4)(functools.partial(add, n=n))
 
         @pl.when(q < HEAD)
         def _():
@@ -443,6 +442,8 @@
             out_ref[0:BLOCK, :] = jnp.zeros((BLOCK, wide), F32)
             out_ref[0:BLOCK, 0:BLOCK] = own_ref[...]
 
+    vmem = pl.BlockSpec(memory_space=pltpu.VMEM)
+
     def whole(*shape):
         return pl.BlockSpec(shape, lambda i: (0,) * len(shape), pipeline_mode=pl.Buffered(1))
 
@@ -452,19 +453,17 @@
         grid=(12 // group,),
         in_specs=[
             pl.BlockSpec(memory_space=pltpu.SMEM),
-            whole(wide, size),
-            whole(wide, size),
+            vmem,
+            vmem,
             whole(BLOCK, BLOCK),
             whole(96, BLOCK),
-            *[whole(2, 4, 2, BLOCK, BLOCK)] * 4,
+            *[vmem] * 8,
             pl.BlockSpec((16, group // 2, BLOCK, BLOCK), lambda i: (0, i, 0, 0)),
             pl.BlockSpec((group * BLOCK, wide), lambda i: (i, 0)),
         ],
         out_specs=pl.BlockSpec((group * BLOCK, wide), lambda i: (i, 0)),
-        compiler_params=pltpu.CompilerParams(vmem_limit_bytes=60 * MIB),
-        cost_estimate=pl.CostEstimate(
-            flops=8_000_000_000, bytes_accessed=24 * MIB, transcendentals=0
-        ),
+        compiler_params=pltpu.CompilerParams(vmem_limit_bytes=52 * MIB),
+        cost_estimate=pl.CostEstimate(flops=1, bytes_accessed=1, transcendentals=0),
         name="finish",
     )(child_map, *solved, own, diagonal, *arrived, row_panel, front)
 
@@ -517,26 +516,47 @@
 
 
 def per_device(front, diagonal, child, child_map):
+    x = lax.axis_index("pcol") // 4
     child_map = child_map.reshape(128)
     diagonal = diagonal.reshape(96, BLOCK)
-    sent = pack_rows(child, child_map).reshape(64, BLOCK, BLOCK)
-    sent = lax.all_to_all(sent, BOTH, 0, 0, axis_index_groups=PLANE_GROUPS, tiled=True)
-    sent = sent.reshape(4, 2, 4, 2, BLOCK, BLOCK)
-    *terms, head_terms = panel_terms(front, diagonal, sent, child_map)
+
+    def exchange(sent):
+        sent = lax.all_to_all(
+            sent.reshape(32, BLOCK, BLOCK), BOTH, 0, 0, axis_index_groups=PLANE_GROUPS, tiled=True
+        )
+        return sent.reshape(4, 2, 4, BLOCK, BLOCK)
+
+    def collect(terms, n):
+        parts = [terms[0]]
+        for d in (1, 2, 3):
+            pairs = [pair for pair in ahead_x(d) if pair[1] // 8 == n]
+            parts.append(lax.ppermute(terms[d], "pcol", pairs))
+        return parts
+
+    def forward(blocks):
+        return [blocks[0]] + [lax.ppermute(blocks[d], "pcol", ahead_x(d)) for d in (1, 2, 3)]
+
+    even, odd = pack_rows(child, child_map)
+    even = exchange(even)
+    even, odd = lax.optimization_barrier((even, odd))
+    odd = exchange(odd)
+    *terms, head_terms = panel_terms(front, diagonal, even, child_map, 0)
     summed, along_z, twins = gather_head(head_terms)
-    summed, *terms = lax.optimization_barrier([summed, *terms])
-    behind = [lax.ppermute(terms[d], "pcol", ahead_x(d)) for d in (1, 2, 3)]
-    behind, along_z = lax.optimization_barrier((behind, along_z))
-    piece = terms[0] + behind[0] + behind[1] + behind[2]
-    gathered = along_z + twins
-    blocks = pack_cols(sent, child_map)
-    piece, *ahead = lax.optimization_barrier([piece, *blocks[1:]])
-    arrived = [blocks[0]]
-    for d in (1, 2, 3):
-        arrived.append(lax.ppermute(ahead[d - 1], "pcol", ahead_x(d)))
+    parts = collect(terms, 0)
+    first = parts[0] + parts[1] + parts[2] + parts[3]
+    first, *blocks = lax.optimization_barrier([first, *pack_cols(even, child_map)])
+    arrived = forward(blocks)
+    odd, arrived, along_z = lax.optimization_barrier((odd, arrived, along_z))
+    *terms, _ = panel_terms(front, diagonal, odd, child_map, 1)
+    parts = collect(terms, 1)
+    *inverse, own = head_factor(along_z + twins)
+    parts, inverse = lax.optimization_barrier((parts, inverse))
+    second = parts[0] + parts[1] + parts[2] + parts[3]
+    piece = jnp.where(x < 2, first, second)
     row_panel = lax.all_gather(piece, "pcol")
     col_panel = gather_columns(piece)
-    *inverse, own = head_factor(gathered)
+    piece, *blocks = lax.optimization_barrier([piece, *pack_cols(odd, child_map)])
+    arrived = arrived + forward(blocks)
     solved = solve_columns(col_panel, inverse)
     return finish(front, diagonal, arrived, row_panel, solved, own, child_map)
 

time: 419 us -> 445 us (1.062)
  blocking collectives: 59.4 us -> 36.7 us
  starting transfers between devices: 60.5 us -> 80.1 us
  local copies, waits for them, and re-layouts: 8.28 us -> 21.7 us
  waiting for transfers between devices: 60.9 us -> 71.5 us
    all_to_all x1, blocking collectives: 59.4 us -> 36.7 us  [exchange(): lax.all_to_all(sent.reshape(32, BLOCK, BLOCK), BOTH, 0, 0, axis_index_gro...]
    ppermute x6 -> x12, starting transfers between devices: 12.4 us -> 27.3 us  [the longest x6 15.1 us: collect(): parts.append(lax.ppermute(terms[d], 'pcol', pairs))]
    unnamed x24 -> x44, local copies, waits for them, and re-layouts: 7.52 us -> 21 us
    ppermute x3, waiting for transfers between devices: 1.12 us -> 11.9 us  [gather_head(): lax.ppermute(held, 'prow', ahead_z(d))]
    ppermute x3, waiting for transfers between devices: 3.87 us -> 11.8 us  [gather_head(): along_y = [held] + [lax.ppermute(held, BOTH, ahead_y(d)) for d in (1, 2, 3)]]
    ppermute x6 -> x12, waiting for transfers between devices: 11.2 us -> 5.02 us  [the longest x6 5 us: forward(): lax.ppermute(blocks[d], 'pcol', ahead_x(d))]
  transfers between devices with their start and end apart: 25 -> 32, of which waited for: 14 -> 10; matrix products, arithmetic and copies ran while one was open for 0% -> 0% of each run, Pallas kernels for 46% -> 45%
where the time goes in v3:
time: 445 us; the launch traced here: 442 us
  Pallas kernels  216 us (49%)
  starting transfers between devices  80.1 us (18%)
  waiting for transfers between devices  71.5 us (16%)
  blocking collectives  36.7 us (8%)
  local copies, waits for them, and re-layouts  21.7 us (5%)
  between operations  13.7 us (3%)
    pallas_call x1, Pallas kernels, head_factor(): pl.pallas_call(kernel, out_shape=[jax.ShapeDtypeStruct((size, size), BF16...  184 us
    all_to_all x1, blocking collectives, exchange(): lax.all_to_all(sent.reshape(32, BLOCK, BLOCK), BOTH, 0, 0, axis_index_gro...  36.7 us
    ppermute x3, waiting for transfers between devices, gather_columns(): return [held] + [lax.ppermute(held, 'prow', ahead_z(d)) for d in (1, 2, 3)]  23.7 us
    ppermute x1, starting transfers between devices, gather_columns(): other = lax.ppermute(turned, 'prow', [(p, p ^ 4) for p in range(8)])  22.5 us
    unnamed x44, local copies, waits for them, and re-layouts  21 us
    ppermute x1, waiting for transfers between devices, gather_columns(): other = lax.ppermute(turned, 'prow', [(p, p ^ 4) for p in range(8)])  16.8 us
    pallas_call x1, Pallas kernels, finish(): pl.pallas_call(kernel, out_shape=jax.ShapeDtypeStruct((12 * BLOCK, wide),...  16 us
    ppermute x6, starting transfers between devices, collect(): parts.append(lax.ppermute(terms[d], 'pcol', pairs))  15.1 us
  transfers between devices with their start and end apart: 32, of which 10 were waited for; matrix products, arithmetic and copies ran while one was open for 0% of the time, Pallas kernels for 45%

profile of v3, /device:TPU:0, one launch (start us, length us, event | category | flops | bytes accessed | tf_op | source)
XLA Modules:
  0.0 442.2 jit_solution(18138691851042014884)
XLA Ops:
  7.3 2.2 copy-done.3
  9.5 2.5 pack_rows.1
  12.0 36.7 %all_to_all.10 = f32[32,128,128]{2,1,0:T(8,128)} all-to-all(f32[32,128,128]{2,1,0:T(8,128)S(1)} %bitcast.13), channel_id=1, replica_groups={{0,16,32,48,64,80,96,112,1,17,33,49,65,81,97,113,2,18,34,50,66,82,98,11..., dimensions={0} | all-to-all | bytes 4194304 | tf_op jit(solution)/shard_map/all_to_all | solution.py:524
  48.7 4.2 all-to-all-start.1
  52.9 2.3 copy-done
  59.4 3.0 collective-permute-start.7
  63.5 2.8 collective-permute-start
  66.3 2.2 collective-permute-done.7
  68.6 3.2 collective-permute-start.10
  75.8 6.7 %collective-permute-done.10 = f32[2,128,128]{2,1,0:T(8,128)S(1)} collective-permute-done((f32[2,128,128]{2,1,0:T(8,128)S(1)}, f32[2,128,128]{2,1,0:T(8,128)S(1)}, u32[]{:S(2)}, u32[]{:S(2)}) %collective-permute-start.10) | collective-permute-done | bytes 131104 | tf_op jit(solution)/shard_map/ppermute | solution.py:498
  83.9 4.9 %collective-permute-done.9 = f32[2,128,128]{2,1,0:T(8,128)S(1)} collective-permute-done((f32[2,128,128]{2,1,0:T(8,128)S(1)}, f32[2,128,128]{2,1,0:T(8,128)S(1)}, u32[]{:S(2)}, u32[]{:S(2)}) %collective-permute-start.9) | collective-permute-done | bytes 131104 | tf_op jit(solution)/shard_map/ppermute | solution.py:498
  90.5 3.0 collective-permute-start.13
  98.0 2.7 collective-permute-start.4
  100.8 3.3 collective-permute-done.12.refs_1_
  104.1 2.8 collective-permute-start.5
  106.8 8.5 %collective-permute-done.13.refs_2_ = f32[8,128,128]{2,1,0:T(8,128)} collective-permute-done((f32[8,128,128]{2,1,0:T(8,128)S(1)}, f32[8,128,128]{2,1,0:T(8,128)}, u32[]{:S(2)}, u32[]{:S(2)}) %collective-permute-start.13) | collective-permute-done | bytes 524320 | tf_op jit(solution)/shard_map/ppermute | solution.py:500
  116.7 5.0 %collective-permute-done.4.refs_2_ = f32[2,4,128,128]{3,2,1,0:T(8,128)S(1)} collective-permute-done((f32[2,4,128,128]{3,2,1,0:T(8,128)S(1)}, f32[2,4,128,128]{3,2,1,0:T(8,128)S(1)}, u32[]{:S(2)}, u32[]{:S(2)}) %collective-permute-start.4) | collective-permute-done | bytes 524320 | tf_op jit(solution)/shard_map/ppermute | solution.py:537
  122.5 2.3 copy-done.1
  124.8 2.1 panel_terms.3
  129.1 6.3 %collective-permute-start.16 = (f32[6,128,128]{2,1,0:T(8,128)}, f32[6,128,128]{2,1,0:T(8,128)}, u32[]{:S(2)}, u32[]{:S(2)}) collective-permute-start(f32[6,128,128]{2,1,0:T(8,128)} %get-tuple-element.75), channel_id=1, source_target_pairs={{0,8},{1,9},{2,10},{3,11},{4,12},{5,13},{6,14},{7,15},{16,24},{17,... | collective-permute-start | bytes 1179656 | tf_op jit(solution)/shard_map/ppermute | solution.py:533
  135.5 2.0 collective-permute-start.17
  137.5 183.7 %head_factor.1 = (bf16[1024,1024]{1,0:T(8,128)(2,1)S(1)}, bf16[1024,1024]{1,0:T(8,128)(2,1)S(1)}, f32[128,128]{1,0:T(8,128)S(1)}) custom-call(f32[8,128,128]{2,1,0:T(8,128)S(1)} %pad_maximum_fusion.1.refs_0_, f32[8,128,128]{2,1,0:T(8,128)} %collective-permute-done.12.refs_1_, f32[8,128,128]{2,1,0:T(8,128)} %collective-permute-done.13.refs_2_, ...), custom_call_target="tpu_custom_call" | custom-call | flops 1 | bytes 1 | tf_op jit(solution)/shard_map/head_factor/pallas_call | solution.py:332
  324.0 2.1 add_select_fusion
  327.9 22.5 %collective-permute-start.23 = (f32[6,128,128]{2,1,0:T(8,128)S(1)}, f32[6,128,128]{2,1,0:T(8,128)S(1)}, u32[]{:S(2)}, u32[]{:S(2)}) collective-permute-start(f32[6,128,128]{2,1,0:T(8,128)S(1)} %collective-permute-done.22), channel_id=1, source_target_pairs={{0,64},{16,80},{32,96},{48,112},{64,0},{80,16},{96,32},{112,48},{1... | collective-permute-start | bytes 1179656 | tf_op jit(solution)/shard_map/ppermute | solution.py:513
  350.4 16.8 %collective-permute-done.23 = f32[6,128,128]{2,1,0:T(8,128)S(1)} collective-permute-done((f32[6,128,128]{2,1,0:T(8,128)S(1)}, f32[6,128,128]{2,1,0:T(8,128)S(1)}, u32[]{:S(2)}, u32[]{:S(2)}) %collective-permute-start.23) | collective-permute-done | bytes 393248 | tf_op jit(solution)/shard_map/ppermute | solution.py:513
  367.9 3.5 collective-permute-start.25
  371.4 2.5 collective-permute-start.26
  375.9 3.3 collective-permute-start.28
  379.3 8.2 %collective-permute-done.24.in1 = f32[2,6,128,128]{3,2,1,0:T(8,128)S(1)} collective-permute-done((f32[2,6,128,128]{3,2,1,0:T(8,128)S(1)}, f32[2,6,128,128]{3,2,1,0:T(8,128)S(1)}, u32[]{:S(2)}, u32[]{:S(2)}) %collective-permute-start.24) | collective-permute-done | bytes 786464 | tf_op jit(solution)/shard_map/ppermute | solution.py:515
  389.3 15.6 %collective-permute-done.25.in2 = f32[2,6,128,128]{3,2,1,0:T(8,128)S(1)} collective-permute-done((f32[2,6,128,128]{3,2,1,0:T(8,128)S(1)}, f32[2,6,128,128]{3,2,1,0:T(8,128)S(1)}, u32[]{:S(2)}, u32[]{:S(2)}) %collective-permute-start.25) | collective-permute-done | bytes 786464 | tf_op jit(solution)/shard_map/ppermute | solution.py:515
  406.4 7.7 %solve_columns.1 = (bf16[768,1024]{1,0:T(8,128)(2,1)S(1)}, bf16[768,1024]{1,0:T(8,128)(2,1)S(1)}) custom-call(bf16[1024,1024]{1,0:T(8,128)(2,1)S(1)} %copy-done.5, bf16[1024,1024]{1,0:T(8,128)(2,1)S(1)} %copy-done.7, f32[2,6,128,128]{3,2,1,0:T(8,128)S(1)} %pad_maximum_fusion.in0, f32[2,6,128,128]{3,2,1,0:T(8,128)S(1)} %collective-permute-done.24.in1, ...), custom_call_target="tpu_custom_call" | custom-call | flops 1 | bytes 1 | tf_op jit(solution)/shard_map/solve_columns/pallas_call | solution.py:378
  419.3 16.0 %finish.1 = f32[1536,768]{1,0:T(8,128)} custom-call(s32[128]{0:T(128)S(1)} %reshape.18.map_ref, bf16[768,1024]{1,0:T(8,128)(2,1)} %copy-done.9, bf16[768,1024]{1,0:T(8,128)(2,1)} %copy-done.10, f32[128,128]{1,0:T(8,128)S(1)} %get-tuple-element.92.own_ref, f32[96,128]{1,0:T(8,128)S(1)} %bitcast.16, f32[2,4,128,128]{3,2,1,0:T(8,128)S(1)} %get-tuple-element.93.refs_0_, ...), custom_call_target="tpu_custom_call" | custom-call | flops 1 | bytes 1 | tf_op jit(solution)/shard_map/finish/pallas_call | solution.py:450
  (92 shorter events, 37.7 us)
Async XLA Ops:
  48.7 73.8 %all-to-all-start.1 = ((f32[32,128,128]{2,1,0:T(8,128)}), f32[32,128,128]{2,1,0:T(8,128)S(1)}, u32[]{:S(2)}, u32[]{:S(2)}) async-start(f32[32,128,128]{2,1,0:T(8,128)} %bitcast.12), calls=%async_computation.1 | async-start | bytes 4194304 | tf_op jit(solution)/shard_map/all_to_all | solution.py:524
  52.9 365.4 %all-gather.3.cloned.1.call-start = ((), (), s32[]{:S(2)}) async-start(), calls=%async_computation.2 | async-start | bytes 6684672 | tf_op jit(solution)/shard_map/all_gather | solution.py:556
  58.0 8.3 %collective-permute-start.6 = (f32[2,128,128]{2,1,0:T(8,128)S(1)}, f32[2,128,128]{2,1,0:T(8,128)S(1)}, u32[]{:S(2)}, u32[]{:S(2)}) collective-permute-start(f32[2,128,128]{2,1,0:T(8,128)S(1)} %get-tuple-element.71), channel_id=1, source_target_pairs={{0,4},{1,5},{2,6},{3,7},{4,8},{5,9},{6,10},{7,11},{8,12},{9,13},{1... | collective-permute-start | bytes 393224 | tf_op jit(solution)/shard_map/ppermute | solution.py:496
  59.4 9.2 %collective-permute-start.7 = (f32[2,128,128]{2,1,0:T(8,128)S(1)}, f32[2,128,128]{2,1,0:T(8,128)S(1)}, u32[]{:S(2)}, u32[]{:S(2)}) collective-permute-start(f32[2,128,128]{2,1,0:T(8,128)S(1)} %get-tuple-element.71), channel_id=1, source_target_pairs={{0,8},{1,9},{2,10},{3,11},{4,12},{5,13},{6,14},{7,15},{8,0},{9,1},... | collective-permute-start | bytes 393224 | tf_op jit(solution)/shard_map/ppermute | solution.py:496
  62.4 6.2 %collective-permute-start.8 = (f32[2,128,128]{2,1,0:T(8,128)S(1)}, f32[2,128,128]{2,1,0:T(8,128)S(1)}, u32[]{:S(2)}, u32[]{:S(2)}) collective-permute-start(f32[2,128,128]{2,1,0:T(8,128)S(1)} %get-tuple-element.71), channel_id=1, source_target_pairs={{0,12},{1,13},{2,14},{3,15},{4,0},{5,1},{6,2},{7,3},{8,4},{9,5},{1... | collective-permute-start | bytes 393224 | tf_op jit(solution)/shard_map/ppermute | solution.py:496
  63.5 30.0 %collective-permute-start = (f32[6,128,128]{2,1,0:T(8,128)S(1)}, f32[6,128,128]{2,1,0:T(8,128)S(1)}, u32[]{:S(2)}, u32[]{:S(2)}) collective-permute-start(f32[6,128,128]{2,1,0:T(8,128)S(1)} %get-tuple-element.60), channel_id=1, source_target_pairs={{0,4},{1,5},{2,6},{3,7},{12,0},{13,1},{14,2},{15,3},{16,20},{17,21... | collective-permute-start | bytes 1179656 | tf_op jit(solution)/shard_map/ppermute | solution.py:533
  68.6 14.0 %collective-permute-start.10 = (f32[2,128,128]{2,1,0:T(8,128)S(1)}, f32[2,128,128]{2,1,0:T(8,128)S(1)}, u32[]{:S(2)}, u32[]{:S(2)}) collective-permute-start(f32[2,128,128]{2,1,0:T(8,128)S(1)} %add_add_fusion.1), channel_id=1, source_target_pairs={{0,64},{1,65},{4,68},{5,69},{8,72},{9,73},{12,76},{13,77},{16,80},... | collective-permute-start | bytes 393224 | tf_op jit(solution)/shard_map/ppermute | solution.py:498
  71.8 23.9 %collective-permute-start.1 = (f32[6,128,128]{2,1,0:T(8,128)S(1)}, f32[6,128,128]{2,1,0:T(8,128)S(1)}, u32[]{:S(2)}, u32[]{:S(2)}) collective-permute-start(f32[6,128,128]{2,1,0:T(8,128)S(1)} %get-tuple-element.61), channel_id=1, source_target_pairs={{8,0},{9,1},{10,2},{11,3},{12,4},{13,5},{14,6},{15,7},{24,16},{25,... | collective-permute-start | bytes 1179656 | tf_op jit(solution)/shard_map/ppermute | solution.py:533
  73.1 22.6 %collective-permute-start.2 = (f32[6,128,128]{2,1,0:T(8,128)S(1)}, f32[6,128,128]{2,1,0:T(8,128)S(1)}, u32[]{:S(2)}, u32[]{:S(2)}) collective-permute-start(f32[6,128,128]{2,1,0:T(8,128)S(1)} %get-tuple-element.62), channel_id=1, source_target_pairs={{4,0},{5,1},{6,2},{7,3},{8,4},{9,5},{10,6},{11,7},{20,16},{21,17},... | collective-permute-start | bytes 1179656 | tf_op jit(solution)/shard_map/ppermute | solution.py:533
  74.4 9.5 %collective-permute-start.11 = (f32[2,128,128]{2,1,0:T(8,128)S(1)}, f32[2,128,128]{2,1,0:T(8,128)S(1)}, u32[]{:S(2)}, u32[]{:S(2)}) collective-permute-start(f32[2,128,128]{2,1,0:T(8,128)S(1)} %add_add_fusion.1), channel_id=1, source_target_pairs={{0,66},{1,67},{4,70},{5,71},{8,74},{9,75},{12,78},{13,79},{16,82},... | collective-permute-start | bytes 393224 | tf_op jit(solution)/shard_map/ppermute | solution.py:498
  82.6 6.3 %collective-permute-start.9 = (f32[2,128,128]{2,1,0:T(8,128)S(1)}, f32[2,128,128]{2,1,0:T(8,128)S(1)}, u32[]{:S(2)}, u32[]{:S(2)}) collective-permute-start(f32[2,128,128]{2,1,0:T(8,128)S(1)} %add_add_fusion.1), channel_id=1, source_target_pairs={{0,2},{1,3},{4,6},{5,7},{8,10},{9,11},{12,14},{13,15},{16,18},{17,... | collective-permute-start | bytes 393224 | tf_op jit(solution)/shard_map/ppermute | solution.py:498
  88.9 15.2 %collective-permute-start.12 = (f32[8,128,128]{2,1,0:T(8,128)S(1)}, f32[8,128,128]{2,1,0:T(8,128)}, u32[]{:S(2)}, u32[]{:S(2)}) collective-permute-start(f32[8,128,128]{2,1,0:T(8,128)S(1)} %pad_maximum_fusion.1.refs_0_), channel_id=1, source_target_pairs={{0,16},{16,32},{32,48},{48,0},{64,80},{80,96},{96,112},{112,64},{1... | collective-permute-start | bytes 1572872 | tf_op jit(solution)/shard_map/ppermute | solution.py:500
  90.5 24.8 %collective-permute-start.13 = (f32[8,128,128]{2,1,0:T(8,128)S(1)}, f32[8,128,128]{2,1,0:T(8,128)}, u32[]{:S(2)}, u32[]{:S(2)}) collective-permute-start(f32[8,128,128]{2,1,0:T(8,128)S(1)} %pad_maximum_fusion.1.refs_0_), channel_id=1, source_target_pairs={{0,32},{16,48},{32,0},{48,16},{64,96},{80,112},{96,64},{112,80},{1... | collective-permute-start | bytes 1572872 | tf_op jit(solution)/shard_map/ppermute | solution.py:500
  93.5 21.9 %collective-permute-start.14 = (f32[8,128,128]{2,1,0:T(8,128)S(1)}, f32[8,128,128]{2,1,0:T(8,128)}, u32[]{:S(2)}, u32[]{:S(2)}) collective-permute-start(f32[8,128,128]{2,1,0:T(8,128)S(1)} %pad_maximum_fusion.1.refs_0_), channel_id=1, source_target_pairs={{0,48},{16,0},{32,16},{48,32},{64,112},{80,64},{96,80},{112,96},{1... | collective-permute-start | bytes 1572872 | tf_op jit(solution)/shard_map/ppermute | solution.py:500
  96.5 19.4 %collective-permute-start.3 = (f32[2,4,128,128]{3,2,1,0:T(8,128)S(1)}, f32[2,4,128,128]{3,2,1,0:T(8,128)S(1)}, u32[]{:S(2)}, u32[]{:S(2)}) collective-permute-start(f32[2,4,128,128]{3,2,1,0:T(8,128)S(1)} %get-tuple-element.68), channel_id=1, source_target_pairs={{0,4},{1,5},{2,6},{3,7},{4,8},{5,9},{6,10},{7,11},{8,12},{9,13},{1... | collective-permute-start | bytes 1572872 | tf_op jit(solution)/shard_map/ppermute | solution.py:537
  98.0 23.7 %collective-permute-start.4 = (f32[2,4,128,128]{3,2,1,0:T(8,128)S(1)}, f32[2,4,128,128]{3,2,1,0:T(8,128)S(1)}, u32[]{:S(2)}, u32[]{:S(2)}) collective-permute-start(f32[2,4,128,128]{3,2,1,0:T(8,128)S(1)} %get-tuple-element.69), channel_id=1, source_target_pairs={{0,8},{1,9},{2,10},{3,11},{4,12},{5,13},{6,14},{7,15},{8,0},{9,1},... | collective-permute-start | bytes 1572872 | tf_op jit(solution)/shard_map/ppermute | solution.py:537
  104.1 18.4 %collective-permute-start.5 = (f32[2,4,128,128]{3,2,1,0:T(8,128)S(1)}, f32[2,4,128,128]{3,2,1,0:T(8,128)}, u32[]{:S(2)}, u32[]{:S(2)}) collective-permute-start(f32[2,4,128,128]{3,2,1,0:T(8,128)S(1)} %get-tuple-element.70), channel_id=1, source_target_pairs={{0,12},{1,13},{2,14},{3,15},{4,0},{5,1},{6,2},{7,3},{8,4},{9,5},{1... | collective-permute-start | bytes 1572872 | tf_op jit(solution)/shard_map/ppermute | solution.py:537
  115.4 13.8 %collective-permute-start.18 = (f32[8,128,128]{2,1,0:T(8,128)S(1)}, f32[8,128,128]{2,1,0:T(8,128)}, u32[]{:S(2)}, u32[]{:S(2)}) collective-permute-start(f32[8,128,128]{2,1,0:T(8,128)S(1)} %pad_maximum_fusion.1.refs_0_), channel_id=1, source_target_pairs={{0,1},{1,0},{2,3},{3,2},{4,5},{5,4},{6,7},{7,6},{8,9},{9,8},{10,11... | collective-permute-start | bytes 1572872 | tf_op jit(solution)/shard_map/ppermute | solution.py:501
  115.4 20.1 %collective-permute-start.19 = (f32[8,128,128]{2,1,0:T(8,128)}, f32[8,128,128]{2,1,0:T(8,128)}, u32[]{:S(2)}, u32[]{:S(2)}) collective-permute-start(f32[8,128,128]{2,1,0:T(8,128)} %collective-permute-done.12.refs_1_), channel_id=1, source_target_pairs={{0,1},{1,0},{2,3},{3,2},{4,5},{5,4},{6,7},{7,6},{8,9},{9,8},{10,11... | collective-permute-start | bytes 1572872 | tf_op jit(solution)/shard_map/ppermute | solution.py:501
  116.7 20.8 %collective-permute-start.20 = (f32[8,128,128]{2,1,0:T(8,128)}, f32[8,128,128]{2,1,0:T(8,128)}, u32[]{:S(2)}, u32[]{:S(2)}) collective-permute-start(f32[8,128,128]{2,1,0:T(8,128)} %collective-permute-done.13.refs_2_), channel_id=1, source_target_pairs={{0,1},{1,0},{2,3},{3,2},{4,5},{5,4},{6,7},{7,6},{8,9},{9,8},{10,11... | collective-permute-start | bytes 1572872 | tf_op jit(solution)/shard_map/ppermute | solution.py:501
  122.5 15.0 %collective-permute-start.21 = (f32[8,128,128]{2,1,0:T(8,128)}, f32[8,128,128]{2,1,0:T(8,128)}, u32[]{:S(2)}, u32[]{:S(2)}) collective-permute-start(f32[8,128,128]{2,1,0:T(8,128)} %collective-permute-done.14.refs_3_), channel_id=1, source_target_pairs={{0,1},{1,0},{2,3},{3,2},{4,5},{5,4},{6,7},{7,6},{8,9},{9,8},{10,11... | collective-permute-start | bytes 1572872 | tf_op jit(solution)/shard_map/ppermute | solution.py:501
  127.7 196.2 %collective-permute-start.15 = (f32[6,128,128]{2,1,0:T(8,128)}, f32[6,128,128]{2,1,0:T(8,128)}, u32[]{:S(2)}, u32[]{:S(2)}) collective-permute-start(f32[6,128,128]{2,1,0:T(8,128)} %get-tuple-element.74), channel_id=1, source_target_pairs={{4,8},{5,9},{6,10},{7,11},{8,12},{9,13},{10,14},{11,15},{20,24},{2... | collective-permute-start | bytes 1179656 | tf_op jit(solution)/shard_map/ppermute | solution.py:533
  129.1 194.8 %collective-permute-start.16 = (f32[6,128,128]{2,1,0:T(8,128)}, f32[6,128,128]{2,1,0:T(8,128)}, u32[]{:S(2)}, u32[]{:S(2)}) collective-permute-start(f32[6,128,128]{2,1,0:T(8,128)} %get-tuple-element.75), channel_id=1, source_target_pairs={{0,8},{1,9},{2,10},{3,11},{4,12},{5,13},{6,14},{7,15},{16,24},{17,... | collective-permute-start | bytes 1179656 | tf_op jit(solution)/shard_map/ppermute | solution.py:533
  135.5 188.5 %collective-permute-start.17 = (f32[6,128,128]{2,1,0:T(8,128)}, f32[6,128,128]{2,1,0:T(8,128)}, u32[]{:S(2)}, u32[]{:S(2)}) collective-permute-start(f32[6,128,128]{2,1,0:T(8,128)} %get-tuple-element.76), channel_id=1, source_target_pairs={{0,12},{1,13},{2,14},{3,15},{12,8},{13,9},{14,10},{15,11},{16,28},... | collective-permute-start | bytes 1179656 | tf_op jit(solution)/shard_map/ppermute | solution.py:533
  326.1 1.8 collective-permute-start.22
  327.9 39.3 %collective-permute-start.23 = (f32[6,128,128]{2,1,0:T(8,128)S(1)}, f32[6,128,128]{2,1,0:T(8,128)S(1)}, u32[]{:S(2)}, u32[]{:S(2)}) collective-permute-start(f32[6,128,128]{2,1,0:T(8,128)S(1)} %collective-permute-done.22), channel_id=1, source_target_pairs={{0,64},{16,80},{32,96},{48,112},{64,0},{80,16},{96,32},{112,48},{1... | collective-permute-start | bytes 1179656 | tf_op jit(solution)/shard_map/ppermute | solution.py:513
  367.3 20.2 %collective-permute-start.24 = (f32[2,6,128,128]{3,2,1,0:T(8,128)S(1)}, f32[2,6,128,128]{3,2,1,0:T(8,128)S(1)}, u32[]{:S(2)}, u32[]{:S(2)}) collective-permute-start(f32[2,6,128,128]{3,2,1,0:T(8,128)S(1)} %pad_maximum_fusion.in0), channel_id=1, source_target_pairs={{0,16},{16,32},{32,48},{48,0},{64,80},{80,96},{96,112},{112,64},{1... | collective-permute-start | bytes 2359304 | tf_op jit(solution)/shard_map/ppermute | solution.py:515
  367.9 36.9 %collective-permute-start.25 = (f32[2,6,128,128]{3,2,1,0:T(8,128)S(1)}, f32[2,6,128,128]{3,2,1,0:T(8,128)S(1)}, u32[]{:S(2)}, u32[]{:S(2)}) collective-permute-start(f32[2,6,128,128]{3,2,1,0:T(8,128)S(1)} %pad_maximum_fusion.in0), channel_id=1, source_target_pairs={{0,32},{16,48},{32,0},{48,16},{64,96},{80,112},{96,64},{112,80},{1... | collective-permute-start | bytes 2359304 | tf_op jit(solution)/shard_map/ppermute | solution.py:515
  371.4 33.4 %collective-permute-start.26 = (f32[2,6,128,128]{3,2,1,0:T(8,128)S(1)}, f32[2,6,128,128]{3,2,1,0:T(8,128)S(1)}, u32[]{:S(2)}, u32[]{:S(2)}) collective-permute-start(f32[2,6,128,128]{3,2,1,0:T(8,128)S(1)} %pad_maximum_fusion.in0), channel_id=1, source_target_pairs={{0,48},{16,0},{32,16},{48,32},{64,112},{80,64},{96,80},{112,96},{1... | collective-permute-start | bytes 2359304 | tf_op jit(solution)/shard_map/ppermute | solution.py:515
  375.9 40.7 %collective-permute-start.27 = (f32[2,4,128,128]{3,2,1,0:T(8,128)S(1)}, f32[2,4,128,128]{3,2,1,0:T(8,128)S(1)}, u32[]{:S(2)}, u32[]{:S(2)}) collective-permute-start(f32[2,4,128,128]{3,2,1,0:T(8,128)S(1)} %get-tuple-element.102), channel_id=1, source_target_pairs={{0,4},{1,5},{2,6},{3,7},{4,8},{5,9},{6,10},{7,11},{8,12},{9,13},{1... | collective-permute-start | bytes 1572872 | tf_op jit(solution)/shard_map/ppermute | solution.py:537
  375.9 40.7 %collective-permute-start.28 = (f32[2,4,128,128]{3,2,1,0:T(8,128)S(1)}, f32[2,4,128,128]{3,2,1,0:T(8,128)S(1)}, u32[]{:S(2)}, u32[]{:S(2)}) collective-permute-start(f32[2,4,128,128]{3,2,1,0:T(8,128)S(1)} %get-tuple-element.103), channel_id=1, source_target_pairs={{0,8},{1,9},{2,10},{3,11},{4,12},{5,13},{6,14},{7,15},{8,0},{9,1},... | collective-permute-start | bytes 1572872 | tf_op jit(solution)/shard_map/ppermute | solution.py:537
  387.4 30.8 %collective-permute-start.29 = (f32[2,4,128,128]{3,2,1,0:T(8,128)S(1)}, f32[2,4,128,128]{3,2,1,0:T(8,128)}, u32[]{:S(2)}, u32[]{:S(2)}) collective-permute-start(f32[2,4,128,128]{3,2,1,0:T(8,128)S(1)} %get-tuple-element.104), channel_id=1, source_target_pairs={{0,12},{1,13},{2,14},{3,15},{4,0},{5,1},{6,2},{7,3},{8,4},{9,5},{1... | collective-permute-start | bytes 1572872 | tf_op jit(solution)/shard_map/ppermute | solution.py:537
  (22 other events, 557.9 us)
Sparse Core Ops, SparseCore 0:
  326.2 52.8 all-gather.2
